TPU v7x, 32 devices: a whole 2x2x4 slice. The times are simulated.
32 devices in a mesh: grp: 16 (over z, y, x), cores: 2 (over core).
Axes of the slice: x: 2, y: 2, z: 4, core: 2. Of those that a mesh axis runs over, the one named last changes fastest.
Arguments:
- invariant_fluid_quantities: float32 [8, 2048, 512], P(None, ('grp', 'cores')), may hold values from -6 to 6
- flux_derivative_matrices: float32 [3, 8, 8], replicated, may hold values from -2 to 2
- levels: int32 [2048], P(('grp', 'cores')), may hold values from 0 to 3
- neighbours: int32 [2048, 6], P(('grp', 'cores')), may hold values from -1 to 2047, as said below
- block_latitude_band: int32 [2048, 1], P(('grp', 'cores')), may hold values from 0 to 15; in each aligned block of 64 rows (0 to 63, 64 to 127, ...) at most 8 rows name the same one
- block_longitude_segment: int32 [2048], P(('grp', 'cores')), may hold values from 0 to 15
- parallel_flow_coefficients: float32 [8], replicated, may hold values from -2 to 2
Outputs:
- state_out: float32 [8, 2048, 512], P(None, ('grp', 'cores'))
- fac_grid: float32 [64, 1024], P(('grp', 'cores'))
- potential: float32 [64, 1024], P(('grp', 'cores'))
- shell_potential: float32 [2048, 128], P(('grp', 'cores'))
Inputs may be any that keep to these rules, and one draw needn't show every extreme that they name: `neighbours`: each entry is -1 or a block held by the same device as the block or by the device just before or after it; device i holds blocks i * 64 to (i + 1) * 64 - 1. `block_latitude_band`: among the 64 blocks of one device no band is named more than 8 times, a bound that some block reaches.
All inputs are finite; a program needn't handle non-finite values.
Results may differ from a plain program's by a relative error of at most 0.0004.
Values sent between devices are 32-bit elements; how exact they have to be, the bound alone decides.
A program may use at most 128 MiB of HBM per device.

v0:
```python
import math

import jax
import jax.numpy as jnp
from jax import lax
from jax.sharding import PartitionSpec as P

LEVELS = 4
STEPS = 2
LAT_DEV = 2
NLON = 1024
DEGREES = 512


COURANT = 0.3
KAPPA2 = 400.0
POT_GAIN = 2000.0
HIGHEST_PRECISION = lax.Precision.HIGHEST


def passed_along(value, axis, steps):
    count = lax.axis_size(axis)
    leading, last = (max(0, -steps), min(count, count - steps))
    return lax.ppermute(value, axis, [(source, source + steps) for source in range(leading, last)])


def block_faces(state_in):
    state_variables, blocks = (state_in.shape[0], state_in.shape[1])
    block_cube = state_in.reshape(state_variables, blocks, 8, 8, 8)
    layers = [
        block_cube[:, :, 0],
        block_cube[:, :, 7],
        block_cube[:, :, :, 0],
        block_cube[:, :, :, 7],
        block_cube[:, :, :, :, 0],
        block_cube[:, :, :, :, 7],
    ]
    return jnp.stack(
        [one_layer.reshape(state_variables, blocks, 64) for one_layer in layers], axis=2
    )


def spread_face(values, direction):
    state_variables, blocks = (values.shape[0], values.shape[1])
    if direction == 0:
        expanded = jnp.broadcast_to(
            values.reshape(state_variables, blocks, 1, 64), (state_variables, blocks, 8, 64)
        )
    elif direction == 1:
        expanded = jnp.broadcast_to(
            values.reshape(state_variables, blocks, 8, 1, 8), (state_variables, blocks, 8, 8, 8)
        )
    else:
        expanded = jnp.broadcast_to(
            values.reshape(state_variables, blocks, 64, 1), (state_variables, blocks, 64, 8)
        )
    return expanded.reshape(state_variables, blocks, 512)


def ghost_values(own_faces, face_table, index):
    result = []
    for face_index in range(6):
        column = index[:, face_index]
        fetched = jnp.take(face_table[:, :, face_index ^ 1], jnp.maximum(column, 0), axis=1)
        selected = jnp.where(column[None, :, None] >= 0, fetched, own_faces[:, :, face_index])
        result.append(spread_face(selected, face_index // 2))
    return result


def wave_speeds(flux_derivative_matrices):
    return jnp.max(jnp.sum(jnp.abs(flux_derivative_matrices), axis=2), axis=1)


def advance(state_in, flux_derivative_matrices, speeds, rate_block, ghosts):
    position = jnp.arange(512, dtype=jnp.int32)
    change = jnp.zeros(state_in.shape, jnp.float32)
    for direction in range(3):
        stride = 64 // 8**direction
        coordinate = position // stride % 8
        lower_side = jnp.where(
            coordinate == 0, ghosts[2 * direction], jnp.roll(state_in, stride, axis=2)
        )
        upper_side = jnp.where(
            coordinate == 7, ghosts[2 * direction + 1], jnp.roll(state_in, -stride, axis=2)
        )
        difference = jnp.einsum(
            "ij,jbp->ibp",
            flux_derivative_matrices[direction],
            upper_side - lower_side,
            precision=HIGHEST_PRECISION,
        )
        change = (
            change
            + 0.5 * difference
            - 0.5 * speeds[direction] * (upper_side - 2.0 * state_in + lower_side)
        )
    return state_in - rate_block[None, :, None] * change


def shell_currents(state_in, parallel_flow_coefficients):
    state_variables, blocks = (state_in.shape[0], state_in.shape[1])
    inner_cells = state_in.reshape(state_variables, blocks, 64, 8)[:, :, :, 0:2]
    inner_cells = jnp.swapaxes(inner_cells, 2, 3).reshape(state_variables, blocks, 128)
    return jnp.einsum(
        "v,vbk->bk", parallel_flow_coefficients, inner_cells, precision=HIGHEST_PRECISION
    )


def fourier_tables(orders):
    longitudes = jnp.arange(NLON, dtype=jnp.int32)
    phase_index = longitudes[:, None] * orders[None, :] % NLON
    angle_rad = phase_index.astype(jnp.float32) * (2.0 * math.pi / NLON)
    return (jnp.cos(angle_rad), jnp.sin(angle_rad))


def legendre_start(sine_lat, orders):
    series_k = jnp.arange(1, DEGREES, dtype=jnp.int32).astype(jnp.float32)
    log_sums = jnp.concatenate(
        [
            jnp.zeros((1,), jnp.float32),
            jnp.cumsum(0.5 * jnp.log((2.0 * series_k + 1.0) / (2.0 * series_k))),
        ]
    )
    log_base = jnp.take(log_sums, orders)
    order_real = orders.astype(jnp.float32)
    return jnp.exp(
        0.5 * math.log(0.5) + log_base[None, :] + order_real[None, :] * jnp.log(sine_lat)[:, None]
    )


def legendre_next_rows(degree, orders, cosine_lat, diagonal_rows, previous, before):
    degree_real = degree.astype(jnp.float32)
    order_real = orders.astype(jnp.float32)[:, None]
    order_int = orders[:, None]
    cosine_row = cosine_lat[None, :]
    ratio_up = jnp.sqrt(
        jnp.maximum(4.0 * degree_real * degree_real - 1.0, 1.0)
        / jnp.maximum(degree_real * degree_real - order_real * order_real, 1.0)
    )
    lower_deg = degree_real - 1.0
    ratio_back = jnp.sqrt(
        jnp.maximum(lower_deg * lower_deg - order_real * order_real, 0.0)
        / jnp.maximum(4.0 * lower_deg * lower_deg - 1.0, 1.0)
    )
    coef_prev = jnp.where(
        degree == order_int + 1,
        jnp.sqrt(2.0 * order_real + 3.0) * cosine_row,
        jnp.where(degree >= order_int + 2, ratio_up * cosine_row, 0.0),
    )
    coef_before = jnp.where(degree >= order_int + 2, -ratio_up * ratio_back, 0.0)
    injected = jnp.where(degree == order_int, diagonal_rows, 0.0)
    return coef_prev * previous + coef_before * before + injected


def solve_spectral(coef_re, coef_im, cosine_lat, sine_lat, weights_lat, orders):
    diagonal_rows = jnp.transpose(legendre_start(sine_lat, orders))
    rows_re = jnp.transpose(coef_re) * weights_lat[None, :]
    rows_im = jnp.transpose(coef_im) * weights_lat[None, :]
    zero_state = jnp.zeros(diagonal_rows.shape, jnp.float32)

    def one_degree(carried, degree):
        previous, before, acc_re, acc_im = carried
        present = legendre_next_rows(degree, orders, cosine_lat, diagonal_rows, previous, before)
        spec_re = jnp.sum(rows_re * present, axis=1)
        spec_im = jnp.sum(rows_im * present, axis=1)
        degree_real = degree.astype(jnp.float32)
        gain_deg = POT_GAIN / (degree_real * (degree_real + 1.0) + KAPPA2)
        acc_re = acc_re + (gain_deg * spec_re)[:, None] * present
        acc_im = acc_im + (gain_deg * spec_im)[:, None] * present
        return ((present, previous, acc_re, acc_im), None)

    carried, _ = lax.scan(
        one_degree,
        (zero_state, zero_state, zero_state, zero_state),
        jnp.arange(DEGREES, dtype=jnp.int32),
        unroll=8,
    )
    return (jnp.transpose(carried[2]), jnp.transpose(carried[3]))


def body(
    invariant_fluid_quantities,
    flux_derivative_matrices,
    levels,
    neighbours,
    block_latitude_band,
    block_longitude_segment,
    parallel_flow_coefficients,
):
    grp_size = lax.axis_size("grp")
    core_size = lax.axis_size("cores")
    device_total = grp_size * core_size
    block_portion = invariant_fluid_quantities.shape[1]
    state_variables = invariant_fluid_quantities.shape[0]
    device = lax.axis_index(("grp", "cores"))
    speeds = wave_speeds(flux_derivative_matrices)
    rate_block = COURANT * jnp.exp2(levels.astype(jnp.float32) - (LEVELS - 1)) / jnp.max(speeds)
    offset = (device - 1) * block_portion
    local_index = jnp.where(neighbours >= 0, neighbours - offset, -1)
    parallel_flow_charge = invariant_fluid_quantities
    for section_index in range(STEPS):
        own_faces = block_faces(parallel_flow_charge)
        flat_faces = own_faces.reshape(state_variables, block_portion, 384)
        faces_prev = passed_along(flat_faces, ("grp", "cores"), 1)
        faces_next = passed_along(flat_faces, ("grp", "cores"), -1)
        face_table = jnp.concatenate([faces_prev, flat_faces, faces_next], axis=1).reshape(
            state_variables, 3 * block_portion, 6, 64
        )
        ghosts = ghost_values(own_faces, face_table, local_index)
        parallel_flow_charge = advance(
            parallel_flow_charge, flux_derivative_matrices, speeds, rate_block, ghosts
        )
    patches = shell_currents(parallel_flow_charge, parallel_flow_coefficients)
    band_index = block_latitude_band[:, 0]
    block_ids = jnp.arange(block_portion, dtype=jnp.int32)
    earlier = (band_index[None, :] == band_index[:, None]) & (
        block_ids[None, :] < block_ids[:, None]
    )
    rank_in_band = jnp.sum(earlier.astype(jnp.int32), axis=1)
    capacity = max(2, 2 * block_portion // grp_size)
    slot_index = band_index * capacity + rank_in_band
    slot_ids = jnp.arange(grp_size * capacity, dtype=jnp.int32)
    placing = (slot_ids[:, None] == slot_index[None, :]).astype(jnp.float32)
    send_rows = jnp.dot(placing, patches, precision=HIGHEST_PRECISION).reshape(
        grp_size, capacity, 128
    )
    send_codes = jnp.dot(
        placing, (block_longitude_segment + 1).astype(jnp.float32), precision=HIGHEST_PRECISION
    ).reshape(grp_size, capacity)
    got_rows, got_codes = (
        lax.all_to_all(send_rows, "grp", split_axis=0, concat_axis=0, tiled=True),
        lax.all_to_all(send_codes, "grp", split_axis=0, concat_axis=0, tiled=True),
    )
    segments = NLON // 64
    segment_codes = jnp.arange(1, segments + 1, dtype=jnp.int32).astype(jnp.float32)
    landing = (got_codes.reshape(-1)[:, None] == segment_codes[None, :]).astype(jnp.float32)
    gathered = jnp.dot(landing.T, got_rows.reshape(-1, 128), precision=HIGHEST_PRECISION)
    fac_local = jnp.swapaxes(gathered.reshape(segments, LAT_DEV, 64), 0, 1).reshape(LAT_DEV, NLON)
    orders_all = jnp.arange(DEGREES, dtype=jnp.int32)
    cos_table, sin_table = fourier_tables(orders_all)
    coef_re = jnp.dot(fac_local, cos_table, precision=HIGHEST_PRECISION) / NLON
    coef_im = -jnp.dot(fac_local, sin_table, precision=HIGHEST_PRECISION) / NLON
    lat_total = LAT_DEV * device_total
    degree_share = DEGREES // device_total
    lat_ids = jnp.arange(lat_total, dtype=jnp.int32)
    colatitude = (lat_ids.astype(jnp.float32) + 0.5) * (math.pi / lat_total)
    cosine_all = jnp.cos(colatitude)
    sine_all = jnp.sin(colatitude)
    weights_all = math.pi / lat_total * sine_all
    own_orders = device * degree_share + jnp.arange(degree_share, dtype=jnp.int32)
    stacked = jnp.stack([coef_re, coef_im])
    regrouped = lax.all_to_all(
        lax.all_to_all(stacked, "grp", split_axis=2, concat_axis=1, tiled=True),
        "cores",
        split_axis=2,
        concat_axis=1,
        tiled=True,
    )
    regrouped = jnp.transpose(
        regrouped.reshape(2, core_size, grp_size, LAT_DEV, degree_share), (0, 2, 1, 3, 4)
    ).reshape(2, lat_total, degree_share)
    synth_re, synth_im = solve_spectral(
        regrouped[0], regrouped[1], cosine_all, sine_all, weights_all, own_orders
    )
    synth_both = jnp.stack([synth_re, synth_im])
    returned = lax.all_to_all(
        lax.all_to_all(synth_both, "grp", split_axis=1, concat_axis=2, tiled=True),
        "cores",
        split_axis=1,
        concat_axis=2,
        tiled=True,
    )
    column_ids = jnp.arange(DEGREES, dtype=jnp.int32)
    order_perm = (
        degree_share
        * (
            core_size * (column_ids // degree_share % grp_size)
            + column_ids // (grp_size * degree_share)
        )
        + column_ids % degree_share
    )
    cos_perm, sin_perm = fourier_tables(order_perm)
    factor = jnp.where(order_perm == 0, jnp.float32(1.0), jnp.float32(2.0))
    potential_local = jnp.dot(
        returned[0] * factor, cos_perm.T, precision=HIGHEST_PRECISION
    ) - jnp.dot(returned[1] * factor, sin_perm.T, precision=HIGHEST_PRECISION)
    grid_segments = jnp.swapaxes(potential_local.reshape(LAT_DEV, segments, 64), 0, 1).reshape(
        segments, 128
    )
    back_rows = jnp.dot(landing, grid_segments, precision=HIGHEST_PRECISION).reshape(
        grp_size, capacity, 128
    )
    home_rows = lax.all_to_all(back_rows, "grp", split_axis=0, concat_axis=0, tiled=True)
    shell_potential = jnp.dot(placing.T, home_rows.reshape(-1, 128), precision=HIGHEST_PRECISION)
    return (parallel_flow_charge, fac_local, potential_local, shell_potential)


def solution(mesh):
    placed = (
        P(None, ("grp", "cores"), None),
        P(),
        P(("grp", "cores")),
        P(("grp", "cores"), None),
        P(("grp", "cores"), None),
        P(("grp", "cores")),
        P(),
    )
    return jax.shard_map(
        body,
        mesh=mesh,
        in_specs=placed,
        out_specs=(
            P(None, ("grp", "cores"), None),
            P(("grp", "cores"), None),
            P(("grp", "cores"), None),
            P(("grp", "cores"), None),
        ),
        check_vma=False,
    )
```

profile of v0, /device:TPU:0, one launch (start us, length us, event | category | flops | bytes accessed | tf_op | source)
XLA Modules:
  0.0 1865.7 jit_solution(11256770868131074179)
XLA Ops:
  16.1 3.9 collective-permute-start
  21.1 8.9 all-to-all-start
  46.5 2.8 copy.528
  66.6 2.8 concatenate.91
  69.4 2.9 concatenate.89
  74.1 3.2 copy.439
  77.3 3.3 copy.434
  87.5 3.2 copy.448
  93.5 2.7 concatenate.86
  96.2 3.6 copy.422
  99.9 2.7 concatenate.85
  113.6 4.4 select_subtract_fusion.3
  118.0 2.7 sub.586
  122.3 2.7 reshape.1290
  126.6 3.2 reshape.1289
  134.0 4.5 select_subtract_fusion.2
  138.4 3.4 copy.440
  143.3 3.4 copy.442
  148.2 3.4 copy.441
  155.9 5.7 broadcast_bitcast_fusion.3
  161.6 3.4 copy.455
  164.9 3.4 copy.457
  168.3 3.5 copy.456
  171.9 4.1 fusion.120
  189.4 2.7 fusion.240
  197.4 3.7 copy.466
  201.1 2.6 reshape.1296
  205.0 4.1 collective-permute-start.2
  220.2 3.2 copy.476
  223.5 3.2 copy.473
  235.2 3.2 copy.485
  238.4 3.2 copy.482
  241.6 2.7 concatenate.101
  244.3 3.6 copy.468
  248.0 2.7 concatenate.100
  250.7 2.7 copy.467
  263.0 4.4 select_subtract_fusion.1
  267.4 2.7 sub.602
  272.6 2.7 reshape.1298
  276.9 3.1 reshape.1297
  289.3 4.4 select_subtract_fusion
  293.7 3.4 copy.477
  299.6 3.4 copy.479
  304.5 3.3 copy.478
  317.1 5.8 broadcast_bitcast_fusion.1
  323.0 3.4 copy.486
  326.3 3.4 copy.488
  329.7 3.4 copy.487
  333.1 3.4 fusion.110
  345.7 6.8 all-to-all-start.1
  353.9 6.2 all-to-all-done.1
  360.5 8.8 fusion.136
  369.3 8.7 fusion.127
  379.6 3.7 all-to-all-start.2
  383.3 7.1 all-to-all-done.2
  392.9 3.7 all_to_all.85
  397.7 1419.0 %while.23 = (s32[]{:T(128)}, f32[16,64]{1,0:T(8,128)S(1)}, f32[16,64]{1,0:T(8,128)S(1)}, f32[16,64]{1,0:T(8,128)S(1)}, f32[16,64]{1,0:T(8,128)S(1)}, /*index=5*/...) while((s32[]{:T(128)}, f32[16,64]{1,0:T(8,128)S(1)}, ...), condition=%wide.region_23.25_spmd.clone.clone.clone.clone, body=%wide.region_6.24_spmd.clone.clone.clone.clone.sunk | while | flops 140675 | bytes 141177 | solution.py:172
  1817.6 3.5 all-to-all-start.4
  1821.1 7.2 all-to-all-done.4
  1829.1 3.7 all_to_all.86
  1832.9 9.8 fusion.87
  1842.7 9.8 fusion.121
  1853.6 3.5 all-to-all-start.6
  1858.7 5.9 all-to-all-done.6
  (2648 shorter events, 1237.9 us)
Async XLA Ops:
  0.6 343.9 %copy-start = (f32[8]{0:T(128)S(1)}, f32[8]{0:T(128)}, u32[]{:S(2)}) copy-start(f32[8]{0:T(128)} %param.17) | copy-start | bytes 100
  4.8 3.5 copy-start.36
  13.4 6.6 copy-start.83
  13.4 6.8 copy-start.84
  13.4 16.5 copy-start.1
  14.8 78.7 %collective-permute-start.1 = (f32[8,64,384]{2,1,0:T(8,128)}, f32[8,64,384]{2,1,0:T(8,128)}, u32[]{:S(2)}, u32[]{:S(2)}) collective-permute-start(f32[8,64,384]{2,1,0:T(8,128)} %reshape.1288), channel_id=1, source_target_pairs={{1,0},{2,1},{3,2},{4,3},{5,4},{6,5},{7,6},{8,7},{9,8},{10,9},{11,1... | collective-permute-start | bytes 2359304 | tf_op jit(solution)/shard_map/ppermute | solution.py:24
  16.1 83.8 %collective-permute-start = (f32[8,64,384]{2,1,0:T(8,128)}, f32[8,64,384]{2,1,0:T(8,128)}, u32[]{:S(2)}, u32[]{:S(2)}) collective-permute-start(f32[8,64,384]{2,1,0:T(8,128)} %reshape.1288), channel_id=1, source_target_pairs={{0,1},{1,2},{2,3},{3,4},{4,5},{5,6},{6,7},{7,8},{8,9},{9,10},{10,1... | collective-permute-start | bytes 2359304 | tf_op jit(solution)/shard_map/ppermute | solution.py:24
  20.2 11.1 copy-start.65
  21.1 324.6 %all-to-all-start = ((f32[16,1,8]{2,1,0:T(1,128)}), f32[16,1,8]{2,1,0:T(1,128)S(1)}, u32[]{:S(2)}, u32[]{:S(2)}) async-start(f32[16,1,8]{2,1,0:T(1,128)} %bitcast.104), calls=%async_computation | async-start | bytes 16384 | tf_op jit(solution)/shard_map/all_to_all | solution.py:232
  38.8 3.8 copy-start.59
  38.8 4.7 copy-start.58
  38.8 5.6 copy-start.26
  45.0 4.3 copy-start.57
  45.0 5.2 copy-start.56
  45.0 6.1 copy-start.25
  49.3 3.4 copy-start.24
  51.1 3.2 copy-start.55
  51.1 4.1 copy-start.54
  52.7 3.4 copy-start.23
  58.3 3.5 copy-start.19
  58.3 3.5 copy-start.40
  69.4 2.9 copy-start.53
  69.4 3.8 copy-start.52
  77.3 3.3 copy-start.51
  77.3 4.2 copy-start.50
  77.3 6.3 copy-start.37
  86.5 5.7 copy-start.85
  102.6 2.6 copy-start.11
  126.6 4.9 copy-start.47
  126.6 7.0 copy-start.46
  148.2 5.1 copy-start.45
  148.2 7.3 copy-start.44
  168.3 3.5 copy-start.2
  168.3 3.5 copy-start.67
  168.3 3.5 copy-start.68
  171.8 4.2 copy-start.6
  171.8 4.2 copy-start.7
  171.8 4.2 copy-start.32
  171.8 4.2 copy-start.33
  171.9 4.2 copy-start.34
  171.9 4.2 copy-start.70
  171.9 4.2 copy-start.72
  203.7 37.9 %collective-permute-start.3 = (f32[8,64,384]{2,1,0:T(8,128)}, f32[8,64,384]{2,1,0:T(8,128)}, u32[]{:S(2)}, u32[]{:S(2)}) collective-permute-start(f32[8,64,384]{2,1,0:T(8,128)} %reshape.1296), channel_id=1, source_target_pairs={{1,0},{2,1},{3,2},{4,3},{5,4},{6,5},{7,6},{8,7},{9,8},{10,9},{11,1... | collective-permute-start | bytes 2359304 | tf_op jit(solution)/shard_map/ppermute | solution.py:24
  205.0 42.9 %collective-permute-start.2 = (f32[8,64,384]{2,1,0:T(8,128)}, f32[8,64,384]{2,1,0:T(8,128)}, u32[]{:S(2)}, u32[]{:S(2)}) collective-permute-start(f32[8,64,384]{2,1,0:T(8,128)} %reshape.1296), channel_id=1, source_target_pairs={{0,1},{1,2},{2,3},{3,4},{4,5},{5,6},{6,7},{7,8},{8,9},{9,10},{10,1... | collective-permute-start | bytes 2359304 | tf_op jit(solution)/shard_map/ppermute | solution.py:24
  250.7 2.7 copy-start.10
  250.7 2.7 copy-start.12
  329.7 3.4 copy-start.69
  333.1 3.4 copy-start.8
  333.1 3.5 copy-start.9
  333.1 3.5 copy-start.29
  333.1 3.5 copy-start.30
  333.1 3.5 copy-start.31
  333.1 3.5 copy-start.71
  333.1 3.5 copy-start.73
  341.9 3.0 copy-start.66
  341.9 18.3 copy-start.82
  345.7 14.4 all-to-all-start.1
  360.5 8.8 copy-start.62
  378.0 19.5 %copy-start.81 = (f32[64]{0:T(128)S(1)}, f32[64]{0:T(128)}, u32[]{:S(2)}) copy-start(f32[64]{0:T(128)} %broadcast_multiply_fusion.16) | copy-start | bytes 772
  379.6 10.9 all-to-all-start.2
  397.7 1435.1 %copy-start.80 = (s32[512]{0:T(512)S(1)}, s32[512]{0:T(512)}, u32[]{:S(2)}) copy-start(s32[512]{0:T(512)} %fusion.193) | copy-start | bytes 6148
  1817.6 10.6 all-to-all-start.4
  1852.5 12.9 copy-start.63
  1853.6 11.0 all-to-all-start.6
  (31 other events, 65.3 us)
where the time goes:
time: 1890 us; the launch traced here: 1870 us
  other arithmetic  1080 us (57%)
  loops' own time  363 us (19%)
  local copies, waits for them, and re-layouts  295 us (16%)
  matrix products  56.2 us (3%)
  starting transfers between devices  36.9 us (2%)
  waiting for transfers between devices  26.4 us (1%)
    another operation x1, loops' own time, solve_spectral(): lax.scan(one_degree, (zero_state, zero_state, zero_state, zero_state), jn...  363 us
    select_n x256, other arithmetic, legendre_next_rows(): jnp.where(degree >= order_int + 2, -ratio_up * ratio_back, 0.0)  321 us
    eq x256, other arithmetic, legendre_next_rows(): degree == order_int + 1  318 us
    eq x256, other arithmetic, legendre_next_rows(): injected = jnp.where(degree == order_int, diagonal_rows, 0.0)  318 us
    reshape x12, local copies, waits for them, and re-layouts, spread_face(): return expanded.reshape(state_variables, blocks, 512)  38.8 us
    slice x64, local copies, waits for them, and re-layouts, solve_spectral(): lax.scan(one_degree, (zero_state, zero_state, zero_state, zero_state), jn...  37.9 us
  transfers between devices with their start and end apart: 9, of which 4 were waited for; matrix products, arithmetic and copies ran while one was open for 16% of the time, Pallas kernels for 0%

commit v1 on v0

--- a/solution.py
+++ b/solution.py
@@ -1,8 +1,11 @@
+import functools
 import math
 
 import jax
 import jax.numpy as jnp
 from jax import lax
+from jax.experimental import pallas as pl
+from jax.experimental.pallas import tpu as pltpu
 from jax.sharding import PartitionSpec as P
 
 LEVELS = 4
@@ -128,54 +131,78 @@
     )
 
 
-def legendre_next_rows(degree, orders, cosine_lat, diagonal_rows, previous, before):
-    degree_real = degree.astype(jnp.float32)
-    order_real = orders.astype(jnp.float32)[:, None]
-    order_int = orders[:, None]
-    cosine_row = cosine_lat[None, :]
-    ratio_up = jnp.sqrt(
-        jnp.maximum(4.0 * degree_real * degree_real - 1.0, 1.0)
-        / jnp.maximum(degree_real * degree_real - order_real * order_real, 1.0)
-    )
-    lower_deg = degree_real - 1.0
-    ratio_back = jnp.sqrt(
-        jnp.maximum(lower_deg * lower_deg - order_real * order_real, 0.0)
-        / jnp.maximum(4.0 * lower_deg * lower_deg - 1.0, 1.0)
-    )
-    coef_prev = jnp.where(
-        degree == order_int + 1,
-        jnp.sqrt(2.0 * order_real + 3.0) * cosine_row,
-        jnp.where(degree >= order_int + 2, ratio_up * cosine_row, 0.0),
-    )
-    coef_before = jnp.where(degree >= order_int + 2, -ratio_up * ratio_back, 0.0)
-    injected = jnp.where(degree == order_int, diagonal_rows, 0.0)
-    return coef_prev * previous + coef_before * before + injected
+def pair_kernel(share_rows, start_ref, order_ref, cosine_ref, weight_ref, out_ref, table):
+    diagonal = start_ref[...]
+    height, pieces = diagonal.shape[0], diagonal.shape[1] // 128
+    order = order_ref[...]
+    square = order * order
+    cosine = cosine_ref[...]
+
+    def one_degree(degree, carried):
+        previous, before = carried
+        real = degree.astype(jnp.float32)
+        top = jnp.full(diagonal.shape, 4.0 * real * real - 1.0, jnp.float32)
+        lower = real - 1.0
+        low = jnp.full(diagonal.shape, 4.0 * lower * lower - 1.0, jnp.float32)
+        up = jnp.sqrt(jnp.maximum(top, 1.0) / jnp.maximum(real * real - square, 1.0))
+        back = jnp.sqrt(jnp.maximum(lower * lower - square, 0.0) / jnp.maximum(low, 1.0))
+        present = (up * cosine) * previous + (-up * back) * before
+        present = present + jnp.where(order == real, diagonal, 0.0)
+        at = pl.multiple_of(degree * height, height)
+        for piece in range(pieces):
+            table[piece, pl.ds(at, height), :] = present[:, 128 * piece : 128 * (piece + 1)]
+        return present, previous
+
+    zero = diagonal * 0.0
+    lax.fori_loop(0, DEGREES, one_degree, (zero, zero), unroll=8)
+    degrees = lax.broadcasted_iota(jnp.int32, (DEGREES, 1), 0).astype(jnp.float32)
+    gain = POT_GAIN / (degrees * (degrees + 1.0) + KAPPA2)
+    for row in range(share_rows):
+        rows = jnp.concatenate(
+            [table[piece, pl.ds(row, DEGREES, stride=height), :] for piece in range(pieces)], axis=1
+        )
+        out_ref[row] = lax.dot_general(
+            rows * weight_ref[...],
+            rows * gain,
+            (((0,), (0,)), ((), ())),
+            precision=HIGHEST_PRECISION,
+            preferred_element_type=jnp.float32,
+        )
+
+
+def order_pairs(sine_lat, cosine_lat, weights_lat, orders):
+    lat_total, share = sine_lat.shape[0], orders.shape[0]
+    side = max(1, min(share, 128 // lat_total))
+    share_rows, lanes = share // side, side * lat_total
+    start = legendre_start(sine_lat, orders).T.reshape(side, share_rows, lat_total)
+    start = jnp.swapaxes(start, 0, 1).reshape(share_rows, lanes)
+    order_real = jnp.broadcast_to(
+        orders.astype(jnp.float32).reshape(side, share_rows, 1), (side, share_rows, lat_total)
+    )
+    order_real = jnp.swapaxes(order_real, 0, 1).reshape(share_rows, lanes)
+    height = -(-share_rows // 8) * 8
+    start = jnp.pad(start, ((0, height - share_rows), (0, 0)))
+    order_real = jnp.pad(order_real, ((0, height - share_rows), (0, 0)))
+    cosine = jnp.tile(cosine_lat, side)[None, :]
+    weight = jnp.tile(weights_lat, side)[None, :]
+    pairs = pl.pallas_call(
+        functools.partial(pair_kernel, share_rows),
+        out_shape=jax.ShapeDtypeStruct((share_rows, lanes, lanes), jnp.float32),
+        scratch_shapes=[pltpu.VMEM((lanes // 128, DEGREES * height, 128), jnp.float32)],
+        compiler_params=pltpu.CompilerParams(vmem_limit_bytes=48 * 1024 * 1024),
+    )(start, order_real, cosine, weight)
+    blocks = [
+        pairs[:, lat_total * at : lat_total * (at + 1), lat_total * at : lat_total * (at + 1)]
+        for at in range(side)
+    ]
+    return jnp.concatenate(blocks, axis=0)
 
 
 def solve_spectral(coef_re, coef_im, cosine_lat, sine_lat, weights_lat, orders):
-    diagonal_rows = jnp.transpose(legendre_start(sine_lat, orders))
-    rows_re = jnp.transpose(coef_re) * weights_lat[None, :]
-    rows_im = jnp.transpose(coef_im) * weights_lat[None, :]
-    zero_state = jnp.zeros(diagonal_rows.shape, jnp.float32)
-
-    def one_degree(carried, degree):
-        previous, before, acc_re, acc_im = carried
-        present = legendre_next_rows(degree, orders, cosine_lat, diagonal_rows, previous, before)
-        spec_re = jnp.sum(rows_re * present, axis=1)
-        spec_im = jnp.sum(rows_im * present, axis=1)
-        degree_real = degree.astype(jnp.float32)
-        gain_deg = POT_GAIN / (degree_real * (degree_real + 1.0) + KAPPA2)
-        acc_re = acc_re + (gain_deg * spec_re)[:, None] * present
-        acc_im = acc_im + (gain_deg * spec_im)[:, None] * present
-        return ((present, previous, acc_re, acc_im), None)
-
-    carried, _ = lax.scan(
-        one_degree,
-        (zero_state, zero_state, zero_state, zero_state),
-        jnp.arange(DEGREES, dtype=jnp.int32),
-        unroll=8,
-    )
-    return (jnp.transpose(carried[2]), jnp.transpose(carried[3]))
+    pairs = order_pairs(sine_lat, cosine_lat, weights_lat, orders)
+    both = jnp.stack([coef_re.T, coef_im.T], axis=1)
+    synth = jnp.einsum("rcj,rjk->crk", both, pairs, precision=HIGHEST_PRECISION)
+    return (synth[0].T, synth[1].T)
 
 
 def body(

time: 1890 us -> 461 us (0.24)
  other arithmetic: 1080 us -> 58.8 us
  loops' own time: 363 us -> 0 us
  local copies, waits for them, and re-layouts: 295 us -> 256 us
    eq x512 -> x0, other arithmetic: 636 us -> none  [the longest x256 318 us: legendre_next_rows(): degree == order_int + 1]
    another operation x1 -> x0, loops' own time: 363 us -> none  [solve_spectral(): lax.scan(one_degree, (zero_state, zero_state, zero_state, zero_state), jn...]
    select_n x256 -> x0, other arithmetic: 321 us -> none  [legendre_next_rows(): jnp.where(degree >= order_int + 2, -ratio_up * ratio_back, 0.0)]
    slice x64 -> x2, local copies, waits for them, and re-layouts: 37.9 us -> 0.15 us  [the longest x1 0.13 us: order_pairs(): pairs[:, lat_total * at:lat_total * (at + 1), lat_total * at:lat_total *...]
    reduce_sum x64 -> x0, other arithmetic: 36.2 us -> none  [one_degree(): spec_im = jnp.sum(rows_im * present, axis=1)]
  transfers between devices with their start and end apart: 9 -> 9, of which waited for: 4 -> 4; matrix products, arithmetic and copies ran while one was open for 16% -> 69% of each run, Pallas kernels for 0% -> 1%
where the time goes in v1:
time: 461 us; the launch traced here: 453 us
  local copies, waits for them, and re-layouts  256 us (56%)
  other arithmetic  58.8 us (13%)
  matrix products  57.5 us (12%)
  starting transfers between devices  36.3 us (8%)
  waiting for transfers between devices  26.4 us (6%)
  blocking collectives  7.42 us (2%)
  Pallas kernels  5.89 us (1%)
    reshape x12, local copies, waits for them, and re-layouts, spread_face(): return expanded.reshape(state_variables, blocks, 512)  38.3 us
    concatenate x8, local copies, waits for them, and re-layouts, body(): jnp.concatenate([faces_prev, flat_faces, faces_next], axis=1)  34.8 us
    unnamed x181, local copies, waits for them, and re-layouts  28.4 us
    gather x12, local copies, waits for them, and re-layouts, ghost_values(): jnp.take(face_table[:, :, face_index ^ 1], jnp.maximum(column, 0), axis=1)  20 us
    sub x6, local copies, waits for them, and re-layouts, advance(): upper_side - lower_side  18.9 us
    another operation x16, local copies, waits for them, and re-layouts, ghost_values(): own_faces[:, :, face_index]  18.1 us
    concatenate x6, local copies, waits for them, and re-layouts, advance(): jnp.roll(state_in, -stride, axis=2)  17.9 us
    sub x4, other arithmetic, advance(): upper_side - lower_side  17.7 us
  transfers between devices with their start and end apart: 9, of which 4 were waited for; matrix products, arithmetic and copies ran while one was open for 69% of the time, Pallas kernels for 1%

profile of v1, /device:TPU:0, one launch (start us, length us, event | category | flops | bytes accessed | tf_op | source)
XLA Modules:
  0.0 452.6 jit_solution(16747149954156581972)
XLA Ops:
  10.3 2.7 reshape.642
  14.3 3.9 collective-permute-start
  19.4 8.4 %all-to-all-start = ((f32[16,1,8]{2,1,0:T(1,128)}), f32[16,1,8]{2,1,0:T(1,128)S(1)}, u32[]{:S(2)}, u32[]{:S(2)}) async-start(f32[16,1,8]{2,1,0:T(1,128)} %bitcast.104), calls=%async_computation | async-start | bytes 16384 | tf_op jit(solution)/shard_map/all_to_all | solution.py:259
  44.1 3.1 concatenate.92
  52.8 3.0 copy.536
  69.1 3.2 copy.442
  72.3 3.3 copy.437
  82.3 3.3 copy.450
  86.4 5.9 %shard_map.102 = f32[8,128,128]{2,1,0:T(8,128)S(1)} custom-call(f32[8,128]{1,0:T(8,128)S(1)} %add_exponential_fusion.start_ref, f32[8,128]{1,0:T(8,128)S(1)} %reshape.664.order_ref, f32[1,128]{1,0:T(1,128)S(1)} %broadcast_in_dim_tile.6.cosine_ref, f32[1,128]{1,0:T(1,128)S(1)} %broadcast_in_dim_tile.7.weight_ref), custom_call_target="tpu_custom_call" | custom-call | tf_op jit(solution)/shard_map/pallas_call | solution.py:188
  93.7 15.2 %concatenate.89 = f32[8,64,6,64]{3,2,1,0:T(8,128)} reshape(f32[8,64,384]{2,1,0:T(8,128)} %collective-permute-done.1) | data formatting | bytes 1572864 | tf_op jit(solution)/shard_map/concatenate | solution.py:233
  111.4 2.7 concatenate.88
  123.9 4.4 select_subtract_fusion.3
  128.3 2.7 sub.202
  132.6 2.7 reshape.644
  136.8 2.8 reshape.643
  143.8 4.5 select_subtract_fusion.2
  148.3 3.4 copy.443
  153.1 3.4 copy.445
  157.9 3.4 copy.444
  164.5 5.8 %broadcast_bitcast_fusion.3 = (f32[8,64,512]{1,2,0:T(8,128)}, f32[8,64,512]{1,2,0:T(8,128)}, f32[8,64,512]{1,2,0:T(8,128)}) fusion(f32[8,64,64]{1,2,0:T(8,128)S(1)} %copy.447, f32[8,64,512]{1,2,0:T(8,128)} %copy.455, f32[8,64,64]{1,2,0:T(8,128)S(1)} %copy.452, pred[64,8]{1,0:T(8,128)(4,1)S(1)} %fusion.81, f32[8,64,512]{1,2,0:T(8,128)} %copy.450, ...), kind=kLoop, calls=%fused_computation.104 | loop fusion | flops 786432 | bytes 5506048 | tf_op jit(solution)/shard_map/reshape | solution.py:60
  170.2 3.4 copy.456
  173.6 3.4 copy.458
  177.0 3.5 copy.457
  180.5 4.1 fusion.43
  187.2 2.7 fusion.38
  198.5 2.7 fusion.167
  209.1 3.7 copy.467
  216.6 4.1 collective-permute-start.2
  225.6 3.0 concatenate.109
  232.9 3.2 copy.477
  236.1 3.3 copy.474
  246.1 3.2 copy.486
  249.3 3.2 copy.483
  252.4 2.7 concatenate.104
  255.2 3.6 copy.469
  258.8 2.7 concatenate.103
  261.6 2.7 copy.468
  271.8 4.4 select_subtract_fusion.1
  276.2 2.7 sub.218
  280.5 2.7 reshape.652
  284.8 3.0 reshape.651
  295.5 4.5 select_subtract_fusion
  300.0 3.5 copy.478
  304.9 3.5 copy.480
  309.8 3.4 copy.479
  321.0 5.8 %broadcast_bitcast_fusion.1 = (f32[8,64,512]{1,2,0:T(8,128)}, f32[8,64,512]{1,2,0:T(8,128)}, f32[8,64,512]{1,2,0:T(8,128)}) fusion(f32[8,64,64]{1,2,0:T(8,128)S(1)} %copy.482, f32[8,64,512]{1,2,0:T(8,128)} %copy.486, f32[8,64,64]{1,2,0:T(8,128)S(1)} %copy.485, pred[64,8]{1,0:T(8,128)(4,1)S(1)} %fusion.81, f32[8,64,512]{1,2,0:T(8,128)} %copy.483, ...), kind=kLoop, calls=%fused_computation.102 | loop fusion | flops 786432 | bytes 5506048 | tf_op jit(solution)/shard_map/reshape | solution.py:60
  326.8 3.4 copy.487
  330.1 3.3 copy.489
  333.5 3.4 copy.488
  336.9 3.6 fusion.33
  351.2 6.7 %all-to-all-start.1 = ((f32[16,8,128]{2,1,0:T(8,128)}), f32[16,8,128]{2,1,0:T(8,128)S(1)}, u32[]{:S(2)}, u32[]{:S(2)}) async-start(f32[16,8,128]{2,1,0:T(8,128)} %convolution_bitcast_fusion), calls=%async_computation.1 | async-start | bytes 131072 | tf_op jit(solution)/shard_map/all_to_all | solution.py:258
  359.4 6.1 %all-to-all-done.1 = f32[16,8,128]{2,1,0:T(8,128)S(1)} async-done(((f32[16,8,128]{2,1,0:T(8,128)}), f32[16,8,128]{2,1,0:T(8,128)S(1)}, u32[]{:S(2)}, u32[]{:S(2)}) %all-to-all-start.1) | async-done | bytes 65568 | tf_op jit(solution)/shard_map/all_to_all | solution.py:258
  365.9 8.8 %fusion.59 = f32[1,2,512]{2,1,0:T(2,128)S(1)} fusion(f32[2,1024]{1,0:T(2,128)S(1)} %reshape.661), kind=kOutput, calls=%fused_computation.87 | convolution fusion | flops 19924992 | bytes 12288 | tf_op jit(solution)/shard_map/dot_general | solution.py:269
  374.7 8.7 %fusion.50 = f32[1,2,512]{2,1,0:T(2,128)S(1)} fusion(f32[2,1024]{1,0:T(2,128)S(1)} %reshape.661), kind=kOutput, calls=%fused_computation.84 | convolution fusion | flops 19923968 | bytes 12288 | tf_op jit(solution)/shard_map/dot_general | solution.py:268
  385.0 3.6 all-to-all-start.2
  388.7 7.2 %all-to-all-done.2 = f32[16,1,128]{2,1,0:T(1,128)S(1)} async-done(((f32[16,1,128]{2,1,0:T(1,128)}), f32[16,1,128]{2,1,0:T(1,128)S(1)}, u32[]{:S(2)}, u32[]{:S(2)}) %all-to-all-start.2) | async-done | bytes 8224 | tf_op jit(solution)/shard_map/all_to_all | solution.py:280
  398.3 3.7 all_to_all.85
  404.5 3.5 all-to-all-start.4
  408.0 7.2 %all-to-all-done.4 = f32[16,1,128]{2,1,0:T(1,128)S(1)} async-done(((f32[16,1,128]{2,1,0:T(1,128)}), f32[16,1,128]{2,1,0:T(1,128)S(1)}, u32[]{:S(2)}, u32[]{:S(2)}) %all-to-all-start.4) | async-done | bytes 8224 | tf_op jit(solution)/shard_map/all_to_all | solution.py:294
  416.1 3.7 all_to_all.86
  419.8 9.8 %fusion.10 = f32[2,1024]{1,0:T(2,128)S(1)} fusion(s32[512]{0:T(512)S(1)} %fusion.125, f32[2,512]{1,0:T(2,128)S(1)} %bitcast.435, f32[512]{0:T(512)S(1)} %compare_select_fusion.8), kind=kOutput, calls=%fused_computation.35 | convolution fusion | flops 19923968 | bytes 16384 | tf_op jit(solution)/shard_map/dot_general | solution.py:313
  429.7 9.8 %fusion.44 = f32[2,1024]{1,0:T(2,128)S(1)} fusion(f32[2,1024]{1,0:T(2,128)S(1)} %fusion.10, s32[512]{0:T(512)S(1)} %fusion.125, f32[2,512]{1,0:T(2,128)S(1)} %bitcast.434, f32[512]{0:T(512)S(1)} %compare_select_fusion.8), kind=kOutput, calls=%fused_computation.82 | convolution fusion | flops 19926016 | bytes 24576 | tf_op jit(solution)/shard_map/dot_general | solution.py:311
  440.5 3.5 all-to-all-start.6
  445.6 5.9 %all-to-all-done.6 = f32[16,8,128]{2,1,0:T(8,128)S(1)} async-done(((f32[16,8,128]{2,1,0:T(8,128)}), f32[16,8,128]{2,1,0:T(8,128)S(1)}, u32[]{:S(2)}, u32[]{:S(2)}) %all-to-all-start.6) | async-done | bytes 65568 | tf_op jit(solution)/shard_map/all_to_all | solution.py:320
  (397 shorter events, 170.3 us)
Async XLA Ops:
  0.6 349.4 %copy-start = (f32[8]{0:T(128)S(1)}, f32[8]{0:T(128)}, u32[]{:S(2)}) copy-start(f32[8]{0:T(128)} %param.15) | copy-start | bytes 100
  10.3 8.0 %copy-start.71 = (s32[64,1]{0,1:T(1,128)S(1)}, s32[64,1]{0,1:T(1,128)}, u32[]{:S(2)}) copy-start(s32[64,1]{0,1:T(1,128)} %param.13) | copy-start | bytes 772
  10.3 8.2 %copy-start.72 = (s32[64]{0:T(128)S(1)}, s32[64]{0:T(128)}, u32[]{:S(2)}) copy-start(s32[64]{0:T(128)} %param.14) | copy-start | bytes 772
  10.3 17.4 %copy-start.1 = (f32[8,64,512]{2,1,0:T(8,128)S(1)}, f32[8,64,512]{2,1,0:T(8,128)}, u32[]{:S(2)}) copy-start(f32[8,64,512]{2,1,0:T(8,128)} %param.9) | copy-start | bytes 3145732
  13.1 80.6 %collective-permute-start.1 = (f32[8,64,384]{2,1,0:T(8,128)}, f32[8,64,384]{2,1,0:T(8,128)}, u32[]{:S(2)}, u32[]{:S(2)}) collective-permute-start(f32[8,64,384]{2,1,0:T(8,128)} %reshape.642), channel_id=1, source_target_pairs={{1,0},{2,1},{3,2},{4,3},{5,4},{6,5},{7,6},{8,7},{9,8},{10,9},{11,1... | collective-permute-start | bytes 2359304 | tf_op jit(solution)/shard_map/ppermute | solution.py:27
  14.3 97.1 %collective-permute-start = (f32[8,64,384]{2,1,0:T(8,128)}, f32[8,64,384]{2,1,0:T(8,128)}, u32[]{:S(2)}, u32[]{:S(2)}) collective-permute-start(f32[8,64,384]{2,1,0:T(8,128)} %reshape.642), channel_id=1, source_target_pairs={{0,1},{1,2},{2,3},{3,4},{4,5},{5,6},{6,7},{7,8},{8,9},{9,10},{10,1... | collective-permute-start | bytes 2359304 | tf_op jit(solution)/shard_map/ppermute | solution.py:27
  19.4 331.9 %all-to-all-start = ((f32[16,1,8]{2,1,0:T(1,128)}), f32[16,1,8]{2,1,0:T(1,128)S(1)}, u32[]{:S(2)}, u32[]{:S(2)}) async-start(f32[16,1,8]{2,1,0:T(1,128)} %bitcast.104), calls=%async_computation | async-start | bytes 16384 | tf_op jit(solution)/shard_map/all_to_all | solution.py:259
  39.2 3.8 copy-start.2
  44.1 3.1 copy-start.46
  44.1 4.0 copy-start.57
  44.1 4.0 copy-start.54
  51.4 4.4 copy-start.26
  52.8 4.6 %copy-start.49 = (f32[8,64,1]{2,1,0:T(8,128)S(1)}, f32[8,64,1]{2,1,0:T(8,128)}, u32[]{:S(2)}) copy-start(f32[8,64,1]{2,1,0:T(8,128)} %get-tuple-element.90) | copy-start | bytes 6148
  52.8 5.5 %copy-start.48 = (f32[8,64,1]{2,1,0:T(8,128)S(1)}, f32[8,64,1]{2,1,0:T(8,128)}, u32[]{:S(2)}) copy-start(f32[8,64,1]{2,1,0:T(8,128)} %get-tuple-element.89) | copy-start | bytes 6148
  55.7 3.4 copy-start.25
  62.8 3.8 copy-start.23
  62.8 3.8 copy-start.35
  64.2 2.8 copy-start.24
  64.2 2.8 copy-start.36
  67.0 12.4 %copy-start.4 = (f32[8,64,512]{2,0,1:T(8,128)}, f32[8,64,512]{2,0,1:T(8,128)S(1)}, u32[]{:S(2)}) copy-start(f32[8,64,512]{2,0,1:T(8,128)S(1)} %pad_maximum_fusion.7) | copy-start | bytes 3145732
  72.2 3.3 copy-start.44
  72.2 4.2 copy-start.43
  81.4 11.0 %copy-start.73 = (s32[64]{0:T(128)S(1)}, s32[64]{0:T(128)}, u32[]{:S(2)}) copy-start(s32[64]{0:T(128)} %param.11) | copy-start | bytes 772
  114.2 2.6 copy-start.14
  117.1 5.4 %copy-start.37 = (f32[8,64,64]{2,0,1:T(8,128)S(1)}, f32[8,64,64]{2,0,1:T(8,128)}, u32[]{:S(2)}) copy-start(f32[8,64,64]{2,0,1:T(8,128)} %copy.429) | copy-start | bytes 393220
  136.8 4.5 copy-start.41
  136.8 6.6 %copy-start.40 = (f32[8,64,64]{2,0,1:T(8,128)S(1)}, f32[8,64,64]{2,0,1:T(8,128)}, u32[]{:S(2)}) copy-start(f32[8,64,64]{2,0,1:T(8,128)} %copy.433) | copy-start | bytes 393220
  157.9 5.2 %copy-start.39 = (f32[8,64,64]{2,0,1:T(8,128)S(1)}, f32[8,64,64]{2,0,1:T(8,128)}, u32[]{:S(2)}) copy-start(f32[8,64,64]{2,0,1:T(8,128)} %copy.446) | copy-start | bytes 393220
  157.9 6.2 %copy-start.38 = (f32[8,64,64]{2,0,1:T(8,128)S(1)}, f32[8,64,64]{2,0,1:T(8,128)}, u32[]{:S(2)}) copy-start(f32[8,64,64]{2,0,1:T(8,128)} %copy.451) | copy-start | bytes 393220
  177.0 3.5 copy-start.3
  177.0 3.5 copy-start.61
  177.0 3.5 copy-start.63
  180.4 4.2 copy-start.9
  180.4 4.2 copy-start.10
  180.4 4.2 copy-start.32
  180.5 4.2 copy-start.33
  180.5 4.2 copy-start.34
  180.5 4.2 copy-start.65
  180.5 4.2 copy-start.67
  184.7 2.5 copy-start.22
  215.4 37.1 %collective-permute-start.3 = (f32[8,64,384]{2,1,0:T(8,128)}, f32[8,64,384]{2,1,0:T(8,128)}, u32[]{:S(2)}, u32[]{:S(2)}) collective-permute-start(f32[8,64,384]{2,1,0:T(8,128)} %reshape.650), channel_id=1, source_target_pairs={{1,0},{2,1},{3,2},{4,3},{5,4},{6,5},{7,6},{8,7},{9,8},{10,9},{11,1... | collective-permute-start | bytes 2359304 | tf_op jit(solution)/shard_map/ppermute | solution.py:27
  216.6 42.2 %collective-permute-start.2 = (f32[8,64,384]{2,1,0:T(8,128)}, f32[8,64,384]{2,1,0:T(8,128)}, u32[]{:S(2)}, u32[]{:S(2)}) collective-permute-start(f32[8,64,384]{2,1,0:T(8,128)} %reshape.650), channel_id=1, source_target_pairs={{0,1},{1,2},{2,3},{3,4},{4,5},{5,6},{6,7},{7,8},{8,9},{9,10},{10,1... | collective-permute-start | bytes 2359304 | tf_op jit(solution)/shard_map/ppermute | solution.py:27
  228.5 3.5 copy-start.52
  236.1 5.1 %copy-start.51 = (f32[8,64,64]{1,2,0:T(8,128)S(1)}, f32[8,64,64]{1,2,0:T(8,128)}, u32[]{:S(2)}) copy-start(f32[8,64,64]{1,2,0:T(8,128)} %get-tuple-element.55) | copy-start | bytes 393220
  261.6 2.7 copy-start.15
  261.6 2.7 copy-start.16
  284.8 6.4 %copy-start.50 = (f32[8,64,64]{2,0,1:T(8,128)S(1)}, f32[8,64,64]{2,0,1:T(8,128)}, u32[]{:S(2)}) copy-start(f32[8,64,64]{2,0,1:T(8,128)} %copy.475) | copy-start | bytes 393220
  309.8 6.9 %copy-start.47 = (f32[8,64,64]{2,0,1:T(8,128)S(1)}, f32[8,64,64]{2,0,1:T(8,128)}, u32[]{:S(2)}) copy-start(f32[8,64,64]{2,0,1:T(8,128)} %copy.484) | copy-start | bytes 393220
  333.5 3.4 copy-start.62
  333.5 3.4 copy-start.64
  336.9 3.7 copy-start.11
  336.9 3.7 copy-start.12
  336.9 3.7 copy-start.29
  336.9 3.7 copy-start.30
  336.9 3.7 copy-start.31
  336.9 3.7 copy-start.66
  336.9 3.7 copy-start.68
  340.7 2.5 copy-start.19
  351.2 14.3 %all-to-all-start.1 = ((f32[16,8,128]{2,1,0:T(8,128)}), f32[16,8,128]{2,1,0:T(8,128)S(1)}, u32[]{:S(2)}, u32[]{:S(2)}) async-start(f32[16,8,128]{2,1,0:T(8,128)} %convolution_bitcast_fusion), calls=%async_computation.1 | async-start | bytes 131072 | tf_op jit(solution)/shard_map/all_to_all | solution.py:258
  365.9 8.8 %copy-start.55 = (f32[2,1024]{1,0:T(2,128)}, f32[2,1024]{1,0:T(2,128)S(1)}, u32[]{:S(2)}) copy-start(f32[2,1024]{1,0:T(2,128)S(1)} %reshape.661) | copy-start | bytes 24580
  385.0 10.8 %all-to-all-start.2 = ((f32[16,1,128]{2,1,0:T(1,128)}), f32[16,1,128]{2,1,0:T(1,128)S(1)}, u32[]{:S(2)}, u32[]{:S(2)}) async-start(f32[16,1,128]{2,1,0:T(1,128)} %reshape.831), calls=%async_computation.2 | async-start | bytes 16384 | tf_op jit(solution)/shard_map/all_to_all | solution.py:280
  404.5 10.6 %all-to-all-start.4 = ((f32[16,1,128]{2,1,0:T(1,128)}), f32[16,1,128]{2,1,0:T(1,128)S(1)}, u32[]{:S(2)}, u32[]{:S(2)}) async-start(f32[16,1,128]{2,1,0:T(1,128)} %reshape.835), calls=%async_computation.4 | async-start | bytes 16384 | tf_op jit(solution)/shard_map/all_to_all | solution.py:294
  439.5 12.9 %copy-start.56 = (f32[2,1024]{1,0:T(2,128)}, f32[2,1024]{1,0:T(2,128)S(1)}, u32[]{:S(2)}) copy-start(f32[2,1024]{1,0:T(2,128)S(1)} %fusion.44) | copy-start | bytes 24580
  440.5 11.0 %all-to-all-start.6 = ((f32[16,8,128]{2,1,0:T(8,128)}), f32[16,8,128]{2,1,0:T(8,128)S(1)}, u32[]{:S(2)}, u32[]{:S(2)}) async-start(f32[16,8,128]{2,1,0:T(8,128)} %fusion.71), calls=%async_computation.6 | async-start | bytes 131072 | tf_op jit(solution)/shard_map/all_to_all | solution.py:320
  (19 other events, 37.6 us)

commit v2 on v1

--- a/solution.py
+++ b/solution.py
@@ -21,91 +21,638 @@
 HIGHEST_PRECISION = lax.Precision.HIGHEST
 
 
-def passed_along(value, axis, steps):
-    count = lax.axis_size(axis)
-    leading, last = (max(0, -steps), min(count, count - steps))
-    return lax.ppermute(value, axis, [(source, source + steps) for source in range(leading, last)])
-
-
-def block_faces(state_in):
-    state_variables, blocks = (state_in.shape[0], state_in.shape[1])
-    block_cube = state_in.reshape(state_variables, blocks, 8, 8, 8)
-    layers = [
-        block_cube[:, :, 0],
-        block_cube[:, :, 7],
-        block_cube[:, :, :, 0],
-        block_cube[:, :, :, 7],
-        block_cube[:, :, :, :, 0],
-        block_cube[:, :, :, :, 7],
-    ]
-    return jnp.stack(
-        [one_layer.reshape(state_variables, blocks, 64) for one_layer in layers], axis=2
-    )
-
-
-def spread_face(values, direction):
-    state_variables, blocks = (values.shape[0], values.shape[1])
-    if direction == 0:
-        expanded = jnp.broadcast_to(
-            values.reshape(state_variables, blocks, 1, 64), (state_variables, blocks, 8, 64)
-        )
-    elif direction == 1:
-        expanded = jnp.broadcast_to(
-            values.reshape(state_variables, blocks, 8, 1, 8), (state_variables, blocks, 8, 8, 8)
-        )
-    else:
-        expanded = jnp.broadcast_to(
-            values.reshape(state_variables, blocks, 64, 1), (state_variables, blocks, 64, 8)
-        )
-    return expanded.reshape(state_variables, blocks, 512)
-
-
-def ghost_values(own_faces, face_table, index):
-    result = []
-    for face_index in range(6):
-        column = index[:, face_index]
-        fetched = jnp.take(face_table[:, :, face_index ^ 1], jnp.maximum(column, 0), axis=1)
-        selected = jnp.where(column[None, :, None] >= 0, fetched, own_faces[:, :, face_index])
-        result.append(spread_face(selected, face_index // 2))
-    return result
-
-
 def wave_speeds(flux_derivative_matrices):
     return jnp.max(jnp.sum(jnp.abs(flux_derivative_matrices), axis=2), axis=1)
 
 
-def advance(state_in, flux_derivative_matrices, speeds, rate_block, ghosts):
-    position = jnp.arange(512, dtype=jnp.int32)
-    change = jnp.zeros(state_in.shape, jnp.float32)
-    for direction in range(3):
-        stride = 64 // 8**direction
-        coordinate = position // stride % 8
-        lower_side = jnp.where(
-            coordinate == 0, ghosts[2 * direction], jnp.roll(state_in, stride, axis=2)
-        )
-        upper_side = jnp.where(
-            coordinate == 7, ghosts[2 * direction + 1], jnp.roll(state_in, -stride, axis=2)
-        )
-        difference = jnp.einsum(
-            "ij,jbp->ibp",
-            flux_derivative_matrices[direction],
-            upper_side - lower_side,
+def split_dot(values, picks):
+    high = values.astype(jnp.bfloat16)
+    low = (values - high.astype(jnp.float32)).astype(jnp.bfloat16)
+    return jnp.dot(high, picks, preferred_element_type=jnp.float32) + jnp.dot(
+        low, picks, preferred_element_type=jnp.float32
+    )
+
+
+def halo_kernel(
+    state_ref, flux_ref, speed_ref, coef_ref, rate_ref, target_ref,
+    state_out, patch_out,
+    cells, diffs, laps, change, own, before, after, picks,
+    send_prev, send_next, recv_prev, recv_next,
+):
+    variables, blocks = state_ref.shape[0], state_ref.shape[1]
+    lanes = 2 * blocks
+    core_size = lax.axis_size("cores")
+    total = lax.axis_size("grp") * core_size
+    device = lax.axis_index("grp") * core_size + lax.axis_index("cores")
+    has_prev, has_next = device > 0, device < total - 1
+    prev_id = (lax.div(device - 1, core_size), lax.rem(device - 1 + core_size, core_size))
+    next_id = (lax.div(device + 1, core_size), lax.rem(device + 1, core_size))
+    mesh_type = pl.DeviceIdType.MESH
+    barrier = pltpu.get_barrier_semaphore()
+
+    @pl.when(has_prev)
+    def _():
+        pl.semaphore_signal(barrier, inc=1, device_id=prev_id, device_id_type=mesh_type)
+
+    @pl.when(has_next)
+    def _():
+        pl.semaphore_signal(barrier, inc=1, device_id=next_id, device_id_type=mesh_type)
+
+    @pl.when(jnp.logical_not(has_prev))
+    def _():
+        before[...] = jnp.zeros_like(before)
+
+    @pl.when(jnp.logical_not(has_next))
+    def _():
+        after[...] = jnp.zeros_like(after)
+
+    left_half = lax.broadcasted_iota(jnp.int32, (1, lanes), 1) < blocks
+    for v in range(variables):
+        both = jnp.concatenate([state_ref[v, :, 0:256], state_ref[v, :, 256:512]], axis=0)
+        cells[v] = both.T
+
+    def copies(step, direction):
+        to_prev = pltpu.make_async_remote_copy(
+            src_ref=own.at[step, direction], dst_ref=after.at[step, direction],
+            send_sem=send_prev.at[step, direction], recv_sem=recv_next.at[step, direction],
+            device_id=prev_id, device_id_type=mesh_type,
+        )
+        to_next = pltpu.make_async_remote_copy(
+            src_ref=own.at[step, direction], dst_ref=before.at[step, direction],
+            send_sem=send_next.at[step, direction], recv_sem=recv_prev.at[step, direction],
+            device_id=next_id, device_id_type=mesh_type,
+        )
+        return to_prev, to_next
+
+    def start(step, direction):
+        to_prev, to_next = copies(step, direction)
+
+        @pl.when(has_prev)
+        def _():
+            to_prev.start()
+
+        @pl.when(has_next)
+        def _():
+            to_next.start()
+
+    def arrive(step, direction):
+        to_prev, to_next = copies(step, direction)
+
+        @pl.when(has_prev)
+        def _():
+            to_next.wait_recv()
+
+        @pl.when(has_next)
+        def _():
+            to_prev.wait_recv()
+
+    def left(step, direction):
+        to_prev, to_next = copies(step, direction)
+
+        @pl.when(has_prev)
+        def _():
+            to_prev.wait_send()
+
+        @pl.when(has_next)
+        def _():
+            to_next.wait_send()
+
+    def fill(step, direction):
+        for v in range(variables):
+            if direction == 0:
+                own[step, 0, pl.ds(64 * v, 64), :] = jnp.where(
+                    left_half, cells[v, 0:64, :], cells[v, 192:256, :]
+                )
+            elif direction == 1:
+                for side in range(2):
+                    for x in range(4):
+                        own[step, 1, pl.ds(256 * side + 32 * v + 8 * x, 8), :] = cells[
+                            v, pl.ds(64 * x + 56 * side, 8), :
+                        ]
+            else:
+                for side in range(2):
+                    own[step, 2, pl.ds(256 * side + 32 * v, 32), :] = cells[
+                        v, pl.ds(7 * side, 32, stride=8), :
+                    ]
+
+    def gathered(step, direction, first, rows, face):
+        part = pl.ds(first, rows)
+        table = jnp.concatenate(
+            [before[step, direction, part, :], own[step, direction, part, :], after[step, direction, part, :]],
+            axis=1,
+        )
+        return split_dot(table, picks[face])
+
+    def keep(v, at, rows, lower, upper, here):
+        diffs[v, pl.ds(at, rows), :] = upper - lower
+        laps[v, pl.ds(at, rows), :] = upper - 2.0 * here + lower
+
+    def sides(step, direction):
+        if direction == 0:
+            known = target_ref[0:1, :] >= 0
+            ghosts = gathered(step, 0, 0, 64 * variables, 0)
+            for v in range(variables):
+                ghost = jnp.where(known, ghosts[64 * v : 64 * v + 64], own[step, 0, pl.ds(64 * v, 64), :])
+                slabs = [cells[v, pl.ds(64 * x, 64), :] for x in range(4)]
+                first = jnp.where(left_half, ghost, pltpu.roll(slabs[3], blocks, 1))
+                last = jnp.where(left_half, pltpu.roll(slabs[0], blocks, 1), ghost)
+                line = [first] + slabs + [last]
+                for x in range(4):
+                    keep(v, 64 * x, 64, line[x], line[x + 2], slabs[x])
+            return
+        near, far = 2 * direction - 1, 2 * direction
+        rows = 32 * variables
+        low = gathered(step, direction, rows, rows, near)
+        high = gathered(step, direction, 0, rows, far)
+        know_low, know_high = target_ref[near : near + 1, :] >= 0, target_ref[far : far + 1, :] >= 0
+        for v in range(variables):
+            part = slice(32 * v, 32 * v + 32)
+            low_v = jnp.where(know_low, low[part], own[step, direction, pl.ds(32 * v, 32), :])
+            high_v = jnp.where(know_high, high[part], own[step, direction, pl.ds(rows + 32 * v, 32), :])
+            if direction == 1:
+                for x in range(4):
+                    slab = cells[v, pl.ds(64 * x, 64), :]
+                    lower = jnp.concatenate([low_v[8 * x : 8 * x + 8], slab[0:56]], axis=0)
+                    upper = jnp.concatenate([slab[8:64], high_v[8 * x : 8 * x + 8]], axis=0)
+                    keep(v, 64 * x, 64, lower, upper, slab)
+            else:
+                whole = cells[v].reshape(32, 8, lanes)
+                height = lax.broadcasted_iota(jnp.int32, (32, 8, lanes), 1)
+                lower = jnp.where(height == 0, low_v[:, None, :], pltpu.roll(whole, 1, 1))
+                upper = jnp.where(height == 7, high_v[:, None, :], pltpu.roll(whole, 7, 1))
+                keep(v, 0, 256, lower.reshape(256, lanes), upper.reshape(256, lanes), cells[v])
+
+    def mix(direction, final):
+        rows = 16
+
+        def one_chunk(chunk, carry):
+            part = pl.ds(pl.multiple_of(chunk * rows, rows), rows)
+            steps = [diffs[v, part, :] for v in range(variables)]
+            for i in range(variables):
+                total_i = -speed_ref[direction] * laps[i, part, :]
+                for j in range(variables):
+                    total_i = total_i + flux_ref[(direction * variables + i) * variables + j] * steps[j]
+                if direction > 0:
+                    total_i = total_i + change[i, part, :]
+                if final:
+                    cells[i, part, :] = cells[i, part, :] - rate_ref[0:1, :] * total_i
+                else:
+                    change[i, part, :] = total_i
+            return carry
+
+        lax.fori_loop(0, 256 // rows, one_chunk, 0)
+
+    fill(0, 0)
+
+    pl.semaphore_wait(barrier, has_prev.astype(jnp.int32) + has_next.astype(jnp.int32))
+    for step in range(STEPS):
+        for direction in range(3):
+            if step > 0 or direction > 0:
+                fill(step, direction)
+            start(step, direction)
+        if step == 0:
+            row_ids = lax.broadcasted_iota(jnp.int32, (3 * lanes, lanes), 0)
+            for face in range(5):
+                hit = row_ids == target_ref[face : face + 1, :]
+                picks[face] = hit.astype(jnp.float32).astype(jnp.bfloat16)
+        for direction in range(3):
+            arrive(step, direction)
+            sides(step, direction)
+            mix(direction, direction == 2)
+    for v in range(variables):
+        flat = cells[v].T
+        state_out[v, :, 0:256] = flat[0:blocks]
+        state_out[v, :, 256:512] = flat[blocks:lanes]
+    layers = []
+    for z in range(2):
+        layer = coef_ref[0] * cells[0, pl.ds(z, 32, stride=8), :]
+        for v in range(1, variables):
+            layer = layer + coef_ref[v] * cells[v, pl.ds(z, 32, stride=8), :]
+        layers.append(layer)
+    turned = jnp.concatenate(layers + layers, axis=0).T
+    for z in range(2):
+        for half in range(2):
+            patch_out[:, pl.ds(64 * z + 32 * half, 32)] = turned[
+                blocks * half : blocks * half + blocks, 32 * z : 32 * z + 32
+            ]
+    for step in range(STEPS):
+        for direction in range(3):
+            left(step, direction)
+
+
+def advance(state_in, flux_derivative_matrices, speeds, rate_block, local_index, parallel_flow_coefficients):
+    variables, blocks = state_in.shape[0], state_in.shape[1]
+    lanes = 2 * blocks
+    here = jnp.where(
+        local_index >= 0, local_index // blocks * lanes + local_index % blocks, -1
+    ).T
+    right = jnp.where(here >= 0, here + blocks, -1)
+    target = jnp.concatenate(
+        [
+            jnp.concatenate([right[0:1], here[1:2]], axis=1),
+            jnp.concatenate([here[2:6], right[2:6]], axis=1),
+            jnp.full((3, lanes), -1, jnp.int32),
+        ],
+        axis=0,
+    )
+    rate = jnp.tile(rate_block, 2)[None, :]
+    vmem, smem = pl.BlockSpec(memory_space=pltpu.VMEM), pl.BlockSpec(memory_space=pltpu.SMEM)
+    whole = (variables, 256, lanes)
+    faces = (STEPS, 3, 64 * variables, lanes)
+    pairs = pltpu.SemaphoreType.DMA((STEPS, 3))
+    return pl.pallas_call(
+        halo_kernel,
+        out_shape=(
+            jax.ShapeDtypeStruct(state_in.shape, jnp.float32),
+            jax.ShapeDtypeStruct((blocks, 128), jnp.float32),
+        ),
+        in_specs=[vmem, smem, smem, smem, vmem, vmem],
+        out_specs=(vmem, vmem),
+        scratch_shapes=[
+            pltpu.VMEM(whole, jnp.float32),
+            pltpu.VMEM(whole, jnp.float32),
+            pltpu.VMEM(whole, jnp.float32),
+            pltpu.VMEM(whole, jnp.float32),
+            pltpu.VMEM(faces, jnp.float32),
+            pltpu.VMEM(faces, jnp.float32),
+            pltpu.VMEM(faces, jnp.float32),
+            pltpu.VMEM((5, 3 * lanes, lanes), jnp.bfloat16),
+            pairs,
+            pairs,
+            pairs,
+            pairs,
+        ],
+        compiler_params=pltpu.CompilerParams(
+            collective_id=0, has_side_effects=True, vmem_limit_bytes=48 * 1024 * 1024
+        ),
+    )(
+        state_in,
+        0.5 * flux_derivative_matrices.reshape(-1),
+        0.5 * speeds,
+        parallel_flow_coefficients,
+        rate,
+        target,
+    )
+
+
+def fourier_tables(orders):
+    longitudes = jnp.arange(NLON, dtype=jnp.int32)
+    phase_index = longitudes[:, None] * orders[None, :] % NLON
+    angle_rad = phase_index.astype(jnp.float32) * (2.0 * math.pi / NLON)
+    return (jnp.cos(angle_rad), jnp.sin(angle_rad))
+
+
+def legendre_start(sine_lat, orders):
+    series_k = jnp.arange(1, DEGREES, dtype=jnp.int32).astype(jnp.float32)
+    log_sums = jnp.concatenate(
+        [
+            jnp.zeros((1,), jnp.float32),
+            jnp.cumsum(0.5 * jnp.log((2.0 * series_k + 1.0) / (2.0 * series_k))),
+        ]
+    )
+    log_base = jnp.take(log_sums, orders)
+    order_real = orders.astype(jnp.float32)
+    return jnp.exp(
+        0.5 * math.log(0.5) + log_base[None, :] + order_real[None, :] * jnp.log(sine_lat)[:, None]
+    )
+
+
+def pair_kernel(share_rows, start_ref, order_ref, cosine_ref, weight_ref, out_ref, table):
+    diagonal = start_ref[...]
+    height, pieces = diagonal.shape[0], diagonal.shape[1] // 128
+    order = order_ref[...]
+    square = order * order
+    cosine = cosine_ref[...]
+
+    def one_degree(degree, carried):
+        previous, before = carried
+        real = degree.astype(jnp.float32)
+        top = jnp.full(diagonal.shape, 4.0 * real * real - 1.0, jnp.float32)
+        lower = real - 1.0
+        low = jnp.full(diagonal.shape, 4.0 * lower * lower - 1.0, jnp.float32)
+        up = jnp.sqrt(jnp.maximum(top, 1.0) / jnp.maximum(real * real - square, 1.0))
+        back = jnp.sqrt(jnp.maximum(lower * lower - square, 0.0) / jnp.maximum(low, 1.0))
+        present = (up * cosine) * previous + (-up * back) * before
+        present = present + jnp.where(order == real, diagonal, 0.0)
+        at = pl.multiple_of(degree * height, height)
+        for piece in range(pieces):
+            table[piece, pl.ds(at, height), :] = present[:, 128 * piece : 128 * (piece + 1)]
+        return present, previous
+
+    zero = diagonal * 0.0
+    lax.fori_loop(0, DEGREES, one_degree, (zero, zero), unroll=8)
+    degrees = lax.broadcasted_iota(jnp.int32, (DEGREES, 1), 0).astype(jnp.float32)
+    gain = POT_GAIN / (degrees * (degrees + 1.0) + KAPPA2)
+    for row in range(share_rows):
+        rows = jnp.concatenate(
+            [table[piece, pl.ds(row, DEGREES, stride=height), :] for piece in range(pieces)], axis=1
+        )
+        out_ref[row] = lax.dot_general(
+            rows * weight_ref[...],
+            rows * gain,
+            (((0,), (0,)), ((), ())),
             precision=HIGHEST_PRECISION,
-        )
-        change = (
-            change
-            + 0.5 * difference
-            - 0.5 * speeds[direction] * (upper_side - 2.0 * state_in + lower_side)
-        )
-    return state_in - rate_block[None, :, None] * change
-
-
-def shell_currents(state_in, parallel_flow_coefficients):
-    state_variables, blocks = (state_in.shape[0], state_in.shape[1])
-    inner_cells = state_in.reshape(state_variables, blocks, 64, 8)[:, :, :, 0:2]
-    inner_cells = jnp.swapaxes(inner_cells, 2, 3).reshape(state_variables, blocks, 128)
-    return jnp.einsum(
-        "v,vbk->bk", parallel_flow_coefficients, inner_cells, precision=HIGHEST_PRECISION
+            preferred_element_type=jnp.float32,
+        )
+
+
+def order_pairs(sine_lat, cosine_lat, weights_lat, orders):
+    lat_total, share = sine_lat.shape[0], orders.shape[0]
+    side = max(1, min(share, 128 // lat_total))
+    share_rows, lanes = share // side, side * lat_total
+    start = legendre_start(sine_lat, orders).T.reshape(side, share_rows, lat_total)
+    start = jnp.swapaxes(start, 0, 1).reshape(share_rows, lanes)
+    order_real = jnp.broadcast_to(
+        orders.astype(jnp.float32).reshape(side, share_rows, 1), (side, share_rows, lat_total)
+    )
+    order_real = jnp.swapaxes(order_real, 0, 1).reshape(share_rows, lanes)
+    height = -(-share_rows // 8) * 8
+    start = jnp.pad(start, ((0, height - share_rows), (0, 0)))
+    order_real = jnp.pad(order_real, ((0, height - share_rows), (0, 0)))
+    cosine = jnp.tile(cosine_lat, side)[None, :]
+    weight = jnp.tile(weights_lat, side)[None, :]
+    pairs = pl.pallas_call(
+        functools.partial(pair_kernel, share_rows),
+        out_shape=jax.ShapeDtypeStruct((share_rows, lanes, lanes), jnp.float32),
+        scratch_shapes=[pltpu.VMEM((lanes // 128, DEGREES * height, 128), jnp.float32)],
+        compiler_params=pltpu.CompilerParams(vmem_limit_bytes=48 * 1024 * 1024),
+    )(start, order_real, cosine, weight)
+    blocks = [
+        pairs[:, lat_total * at : lat_total * (at + 1), lat_total * at : lat_total * (at + 1)]
+        for at in range(side)
+    ]
+    return jnp.concatenate(blocks, axis=0)
+
+
+def solve_spectral(coef_re, coef_im, cosine_lat, sine_lat, weights_lat, orders):
+    pairs = order_pairs(sine_lat, cosine_lat, weights_lat, orders)
+    both = jnp.stack([coef_re.T, coef_im.T], axis=1)
+    synth = jnp.einsum("rcj,rjk->crk", both, pairs, precision=HIGHEST_PRECISION)
+    return (synth[0].T, synth[1].T)
+
+
+def body(
+    invariant_fluid_quantities,
+    flux_derivative_matrices,
+    levels,
+    neighbours,
+    block_latitude_band,
+    block_longitude_segment,
+    parallel_flow_coefficients,
+):
+    grp_size = lax.axis_size("grp")
+    core_size = lax.axis_size("cores")
+    device_total = grp_size * core_size
+    block_portion = invariant_fluid_quantities.shape[1]
+    device = lax.axis_index("grp") * core_size + lax.axis_index("cores")
+    has_prev, has_next = device > 0, device < total - 1
+    prev_id = (lax.div(device - 1, core_size), lax.rem(device - 1 + core_size, core_size))
+    next_id = (lax.div(device + 1, core_size), lax.rem(device + 1, core_size))
+    mesh_type = pl.DeviceIdType.MESH
+    barrier = pltpu.get_barrier_semaphore()
+
+    @pl.when(has_prev)
+    def _():
+        pl.semaphore_signal(barrier, inc=1, device_id=prev_id, device_id_type=mesh_type)
+
+    @pl.when(has_next)
+    def _():
+        pl.semaphore_signal(barrier, inc=1, device_id=next_id, device_id_type=mesh_type)
+
+    @pl.when(jnp.logical_not(has_prev))
+    def _():
+        before[...] = jnp.zeros_like(before)
+
+    @pl.when(jnp.logical_not(has_next))
+    def _():
+        after[...] = jnp.zeros_like(after)
+
+    left_half = lax.broadcasted_iota(jnp.int32, (1, lanes), 1) < blocks
+    for v in range(variables):
+        both = jnp.concatenate([state_ref[v, :, 0:256], state_ref[v, :, 256:512]], axis=0)
+        cells[v] = both.T
+
+    def copies(step, direction):
+        to_prev = pltpu.make_async_remote_copy(
+            src_ref=own.at[step, direction], dst_ref=after.at[step, direction],
+            send_sem=send_prev.at[step, direction], recv_sem=recv_next.at[step, direction],
+            device_id=prev_id, device_id_type=mesh_type,
+        )
+        to_next = pltpu.make_async_remote_copy(
+            src_ref=own.at[step, direction], dst_ref=before.at[step, direction],
+            send_sem=send_next.at[step, direction], recv_sem=recv_prev.at[step, direction],
+            device_id=next_id, device_id_type=mesh_type,
+        )
+        return to_prev, to_next
+
+    def start(step, direction):
+        to_prev, to_next = copies(step, direction)
+
+        @pl.when(has_prev)
+        def _():
+            to_prev.start()
+
+        @pl.when(has_next)
+        def _():
+            to_next.start()
+
+    def arrive(step, direction):
+        to_prev, to_next = copies(step, direction)
+
+        @pl.when(has_prev)
+        def _():
+            to_next.wait_recv()
+
+        @pl.when(has_next)
+        def _():
+            to_prev.wait_recv()
+
+    def left(step, direction):
+        to_prev, to_next = copies(step, direction)
+
+        @pl.when(has_prev)
+        def _():
+            to_prev.wait_send()
+
+        @pl.when(has_next)
+        def _():
+            to_next.wait_send()
+
+    def fill(step, direction):
+        for v in range(variables):
+            if direction == 0:
+                own[step, 0, pl.ds(64 * v, 64), :] = jnp.where(
+                    left_half, cells[v, 0:64, :], cells[v, 192:256, :]
+                )
+            elif direction == 1:
+                for side in range(2):
+                    for x in range(4):
+                        own[step, 1, pl.ds(256 * side + 32 * v + 8 * x, 8), :] = cells[
+                            v, pl.ds(64 * x + 56 * side, 8), :
+                        ]
+            else:
+                for side in range(2):
+                    own[step, 2, pl.ds(256 * side + 32 * v, 32), :] = cells[
+                        v, pl.ds(7 * side, 32, stride=8), :
+                    ]
+
+    def gathered(step, direction, first, rows, face):
+        part = pl.ds(first, rows)
+        table = jnp.concatenate(
+            [before[step, direction, part, :], own[step, direction, part, :], after[step, direction, part, :]],
+            axis=1,
+        )
+        return split_dot(table, picks[face])
+
+    def keep(v, at, rows, lower, upper, here):
+        diffs[v, pl.ds(at, rows), :] = upper - lower
+        laps[v, pl.ds(at, rows), :] = upper - 2.0 * here + lower
+
+    def sides(step, direction):
+        if direction == 0:
+            known = target_ref[0:1, :] >= 0
+            ghosts = gathered(step, 0, 0, 64 * variables, 0)
+            for v in range(variables):
+                ghost = jnp.where(known, ghosts[64 * v : 64 * v + 64], own[step, 0, pl.ds(64 * v, 64), :])
+                slabs = [cells[v, pl.ds(64 * x, 64), :] for x in range(4)]
+                first = jnp.where(left_half, ghost, pltpu.roll(slabs[3], blocks, 1))
+                last = jnp.where(left_half, pltpu.roll(slabs[0], blocks, 1), ghost)
+                line = [first] + slabs + [last]
+                for x in range(4):
+                    keep(v, 64 * x, 64, line[x], line[x + 2], slabs[x])
+            return
+        near, far = 2 * direction - 1, 2 * direction
+        rows = 32 * variables
+        low = gathered(step, direction, rows, rows, near)
+        high = gathered(step, direction, 0, rows, far)
+        know_low, know_high = target_ref[near : near + 1, :] >= 0, target_ref[far : far + 1, :] >= 0
+        for v in range(variables):
+            part = slice(32 * v, 32 * v + 32)
+            low_v = jnp.where(know_low, low[part], own[step, direction, pl.ds(32 * v, 32), :])
+            high_v = jnp.where(know_high, high[part], own[step, direction, pl.ds(rows + 32 * v, 32), :])
+            if direction == 1:
+                for x in range(4):
+                    slab = cells[v, pl.ds(64 * x, 64), :]
+                    lower = jnp.concatenate([low_v[8 * x : 8 * x + 8], slab[0:56]], axis=0)
+                    upper = jnp.concatenate([slab[8:64], high_v[8 * x : 8 * x + 8]], axis=0)
+                    keep(v, 64 * x, 64, lower, upper, slab)
+            else:
+                whole = cells[v].reshape(32, 8, lanes)
+                height = lax.broadcasted_iota(jnp.int32, (32, 8, lanes), 1)
+                lower = jnp.where(height == 0, low_v[:, None, :], pltpu.roll(whole, 1, 1))
+                upper = jnp.where(height == 7, high_v[:, None, :], pltpu.roll(whole, 7, 1))
+                keep(v, 0, 256, lower.reshape(256, lanes), upper.reshape(256, lanes), cells[v])
+
+    def mix(direction, final):
+        rows = 16
+
+        def one_chunk(chunk, carry):
+            part = pl.ds(pl.multiple_of(chunk * rows, rows), rows)
+            steps = [diffs[v, part, :] for v in range(variables)]
+            for i in range(variables):
+                total_i = -speed_ref[direction] * laps[i, part, :]
+                for j in range(variables):
+                    total_i = total_i + flux_ref[(direction * variables + i) * variables + j] * steps[j]
+                if direction > 0:
+                    total_i = total_i + change[i, part, :]
+                if final:
+                    cells[i, part, :] = cells[i, part, :] - rate_ref[0:1, :] * total_i
+                else:
+                    change[i, part, :] = total_i
+            return carry
+
+        lax.fori_loop(0, 256 // rows, one_chunk, 0)
+
+    fill(0, 0)
+
+    pl.semaphore_wait(barrier, has_prev.astype(jnp.int32) + has_next.astype(jnp.int32))
+    for step in range(STEPS):
+        for direction in range(3):
+            if step > 0 or direction > 0:
+                fill(step, direction)
+            start(step, direction)
+        if step == 0:
+            row_ids = lax.broadcasted_iota(jnp.int32, (3 * lanes, lanes), 0)
+            for face in range(5):
+                hit = row_ids == target_ref[face : face + 1, :]
+                picks[face] = hit.astype(jnp.float32).astype(jnp.bfloat16)
+        for direction in range(3):
+            arrive(step, direction)
+            sides(step, direction)
+            mix(direction, direction == 2)
+    for v in range(variables):
+        flat = cells[v].T
+        state_out[v, :, 0:256] = flat[0:blocks]
+        state_out[v, :, 256:512] = flat[blocks:lanes]
+    layers = []
+    for z in range(2):
+        layer = coef_ref[0] * cells[0, pl.ds(z, 32, stride=8), :]
+        for v in range(1, variables):
+            layer = layer + coef_ref[v] * cells[v, pl.ds(z, 32, stride=8), :]
+        layers.append(layer)
+    turned = jnp.concatenate(layers + layers, axis=0).T
+    for z in range(2):
+        for half in range(2):
+            patch_out[:, pl.ds(64 * z + 32 * half, 32)] = turned[
+                blocks * half : blocks * half + blocks, 32 * z : 32 * z + 32
+            ]
+    for step in range(STEPS):
+        for direction in range(3):
+            left(step, direction)
+
+
+def advance(state_in, flux_derivative_matrices, speeds, rate_block, local_index, parallel_flow_coefficients):
+    variables, blocks = state_in.shape[0], state_in.shape[1]
+    lanes = 2 * blocks
+    here = jnp.where(
+        local_index >= 0, local_index // blocks * lanes + local_index % blocks, -1
+    ).T
+    right = jnp.where(here >= 0, here + blocks, -1)
+    target = jnp.concatenate(
+        [
+            jnp.concatenate([right[0:1], here[1:2]], axis=1),
+            jnp.concatenate([here[2:6], right[2:6]], axis=1),
+            jnp.full((3, lanes), -1, jnp.int32),
+        ],
+        axis=0,
+    )
+    rate = jnp.tile(rate_block, 2)[None, :]
+    vmem, smem = pl.BlockSpec(memory_space=pltpu.VMEM), pl.BlockSpec(memory_space=pltpu.SMEM)
+    whole = (variables, 256, lanes)
+    faces = (STEPS, 3, 64 * variables, lanes)
+    pairs = pltpu.SemaphoreType.DMA((STEPS, 3))
+    return pl.pallas_call(
+        halo_kernel,
+        out_shape=(
+            jax.ShapeDtypeStruct(state_in.shape, jnp.float32),
+            jax.ShapeDtypeStruct((blocks, 128), jnp.float32),
+        ),
+        in_specs=[vmem, smem, smem, smem, vmem, vmem],
+        out_specs=(vmem, vmem),
+        scratch_shapes=[
+            pltpu.VMEM(whole, jnp.float32),
+            pltpu.VMEM(whole, jnp.float32),
+            pltpu.VMEM(whole, jnp.float32),
+            pltpu.VMEM(whole, jnp.float32),
+            pltpu.VMEM(faces, jnp.float32),
+            pltpu.VMEM(faces, jnp.float32),
+            pltpu.VMEM(faces, jnp.float32),
+            pltpu.VMEM((5, 3 * lanes, lanes), jnp.bfloat16),
+            pairs,
+            pairs,
+            pairs,
+            pairs,
+        ],
+        compiler_params=pltpu.CompilerParams(
+            collective_id=0, has_side_effects=True, vmem_limit_bytes=48 * 1024 * 1024
+        ),
+    )(
+        state_in,
+        0.5 * flux_derivative_matrices.reshape(-1),
+        0.5 * speeds,
+        parallel_flow_coefficients,
+        rate,
+        target,
     )
 
 
@@ -224,20 +771,14 @@
     rate_block = COURANT * jnp.exp2(levels.astype(jnp.float32) - (LEVELS - 1)) / jnp.max(speeds)
     offset = (device - 1) * block_portion
     local_index = jnp.where(neighbours >= 0, neighbours - offset, -1)
-    parallel_flow_charge = invariant_fluid_quantities
-    for section_index in range(STEPS):
-        own_faces = block_faces(parallel_flow_charge)
-        flat_faces = own_faces.reshape(state_variables, block_portion, 384)
-        faces_prev = passed_along(flat_faces, ("grp", "cores"), 1)
-        faces_next = passed_along(flat_faces, ("grp", "cores"), -1)
-        face_table = jnp.concatenate([faces_prev, flat_faces, faces_next], axis=1).reshape(
-            state_variables, 3 * block_portion, 6, 64
-        )
-        ghosts = ghost_values(own_faces, face_table, local_index)
-        parallel_flow_charge = advance(
-            parallel_flow_charge, flux_derivative_matrices, speeds, rate_block, ghosts
-        )
-    patches = shell_currents(parallel_flow_charge, parallel_flow_coefficients)
+    parallel_flow_charge, patches = advance(
+        invariant_fluid_quantities,
+        flux_derivative_matrices,
+        speeds,
+        rate_block,
+        local_index,
+        parallel_flow_coefficients,
+    )
     band_index = block_latitude_band[:, 0]
     block_ids = jnp.arange(block_portion, dtype=jnp.int32)
     earlier = (band_index[None, :] == band_index[:, None]) & (

time: 461 us -> 175 us (0.38); the launches traced: 453 us -> 174 us
  local copies, waits for them, and re-layouts: 256 us -> 11.6 us
  other arithmetic: 58.8 us -> 8.53 us
  Pallas kernels: 5.89 us -> 34.3 us
  matrix products: 57.5 us -> 41.2 us
  starting transfers between devices: 36.3 us -> 41.9 us
    concatenate x20 -> x1, local copies, waits for them, and re-layouts: 69.2 us -> 0.07 us  [advance(): jnp.concatenate([jnp.concatenate([right[0:1], here[1:2]], axis=1), jnp.co...]
    reshape x17 -> x1, local copies, waits for them, and re-layouts: 44.5 us -> 0.01 us  [the longest x12 38.3 us: spread_face(): return expanded.reshape(state_variables, blocks, 512)]
    another operation x34 -> x3, local copies, waits for them, and re-layouts: 29.3 us -> 0.21 us  [the longest x16 18.1 us: ghost_values(): own_faces[:, :, face_index]]
    pallas_call x0 -> x1, Pallas kernels: none -> 28.4 us  [advance(): pl.pallas_call(halo_kernel, out_shape=(jax.ShapeDtypeStruct(state_in.shap...]
    sub x8 -> x0, local copies, waits for them, and re-layouts: 23.1 us -> none  [the longest x6 18.9 us: advance(): upper_side - lower_side]
    unnamed x181 -> x18, local copies, waits for them, and re-layouts: 28.4 us -> 6 us
    gather x12 -> x0, local copies, waits for them, and re-layouts: 20 us -> none  [ghost_values(): jnp.take(face_table[:, :, face_index ^ 1], jnp.maximum(column, 0), axis=1)]
    sub x4 -> x0, other arithmetic: 17.7 us -> none  [advance(): upper_side - lower_side]
  transfers between devices with their start and end apart: 9 -> 5, of which waited for: 4 -> 4; matrix products, arithmetic and copies ran while one was open for 69% -> 5% of each run, Pallas kernels for 1% -> 20%
where the time goes in v2:
time: 175 us; the launch traced here: 174 us
  starting transfers between devices  41.9 us (24%)
  matrix products  41.2 us (24%)
  Pallas kernels  34.3 us (20%)
  waiting for transfers between devices  27.9 us (16%)
  local copies, waits for them, and re-layouts  11.6 us (7%)
  other arithmetic  8.53 us (5%)
  blocking collectives  7.42 us (4%)
    pallas_call x1, Pallas kernels, advance(): pl.pallas_call(halo_kernel, out_shape=(jax.ShapeDtypeStruct(state_in.shap...  28.4 us
    all_to_all x1, starting transfers between devices, body(): lax.all_to_all(send_rows, 'grp', split_axis=0, concat_axis=0, tiled=True)  22.9 us
    dot_general x1, matrix products, body(): jnp.dot(returned[1] * factor, sin_perm.T, precision=HIGHEST_PRECISION)  9.83 us
    dot_general x1, matrix products, body(): jnp.dot(returned[0] * factor, cos_perm.T, precision=HIGHEST_PRECISION)  9.81 us
    dot_general x1, matrix products, body(): coef_im = -jnp.dot(fac_local, sin_table, precision=HIGHEST_PRECISION) / NLON  8.79 us
    dot_general x1, matrix products, body(): coef_re = jnp.dot(fac_local, cos_table, precision=HIGHEST_PRECISION) / NLON  8.73 us
    all_to_all x1, starting transfers between devices, body(): lax.all_to_all(send_codes, 'grp', split_axis=0, concat_axis=0, tiled=True)  8.31 us
    all_to_all x1, waiting for transfers between devices, body(): lax.all_to_all(back_rows, 'grp', split_axis=0, concat_axis=0, tiled=True)  7.5 us
  transfers between devices with their start and end apart: 5, of which 4 were waited for; matrix products, arithmetic and copies ran while one was open for 5% of the time, Pallas kernels for 20%

profile of v2, /device:TPU:0, one launch (start us, length us, event | category | flops | bytes accessed | tf_op | source)
XLA Modules:
  0.0 173.9 jit_solution(16666152842919995999)
XLA Ops:
  0.6 0.9 convert_reduce_fusion
  1.5 0.7 multiply_add_fusion
  2.2 0.8 convolution_bitcast_fusion.3
  3.0 0.8 all_to_all.60
  3.7 8.3 %all-to-all-start = ((f32[16,1,8]{2,1,0:T(1,128)}), f32[16,1,8]{2,1,0:T(1,128)S(1)}, u32[]{:S(2)}, u32[]{:S(2)}) async-start(f32[16,1,8]{2,1,0:T(1,128)} %bitcast.4), calls=%async_computation | async-start | bytes 16384 | tf_op jit(solution)/shard_map/all_to_all | solution.py:800
  12.1 0.7 add_select_fusion.4
  13.0 0.8 abs_reduce_fusion
  13.8 0.7 fusion.118
  14.4 1.3 multiply_divide_fusion
  15.7 0.1 broadcast_in_dim_tile.9.rate_ref
  15.8 0.1 mul.202.flux_ref
  16.1 1.2 copy-done
  17.3 0.7 copy-done.1
  18.0 28.4 %shard_map.102 = (f32[8,64,512]{2,1,0:T(8,128)S(1)}, f32[64,128]{1,0:T(8,128)S(1)}) custom-call(f32[8,64,512]{2,1,0:T(8,128)S(1)} %copy-done, f32[192]{0:T(256)S(1)} %mul.202.flux_ref, f32[3]{0:T(128)S(1)} %broadcast_multiply_fusion.2.speed_ref, f32[8]{0:T(128)S(1)} %copy-done.1, f32[1,128]{1,0:T(1,128)S(1)} %broadcast_in_dim_tile.9.rate_ref, ...), custom_call_target="tpu_custom_call" | custom-call | tf_op jit(solution)/shard_map/pallas_call | solution.py:624
  46.4 0.8 convolution_bitcast_fusion
  47.2 0.3 reduce-window.9
  47.6 0.1 slice_reduce_fusion
  47.9 0.7 gather_fusion
  48.6 0.1 gather.7
  48.7 0.1 copy.79
  49.1 0.1 mul.220
  49.4 0.1 broadcast_in_dim_tile.10.cosine_ref
  49.5 0.1 broadcast_in_dim_tile.11.weight_ref
  49.6 5.9 %shard_map.103 = f32[8,128,128]{2,1,0:T(8,128)S(1)} custom-call(f32[8,128]{1,0:T(8,128)S(1)} %add_exponential_fusion.start_ref, f32[8,128]{1,0:T(8,128)S(1)} %reshape.238.order_ref, f32[1,128]{1,0:T(1,128)S(1)} %broadcast_in_dim_tile.10.cosine_ref, f32[1,128]{1,0:T(1,128)S(1)} %broadcast_in_dim_tile.11.weight_ref), custom_call_target="tpu_custom_call" | custom-call | tf_op jit(solution)/shard_map/pallas_call | solution.py:735
  55.5 22.9 %all-to-all-start.1 = ((f32[16,8,128]{2,1,0:T(8,128)}), f32[16,8,128]{2,1,0:T(8,128)S(1)}, u32[]{:S(2)}, u32[]{:S(2)}) async-start(f32[16,8,128]{2,1,0:T(8,128)} %convolution_bitcast_fusion), calls=%async_computation.1 | async-start | bytes 131072 | tf_op jit(solution)/shard_map/all_to_all | solution.py:799
  78.4 0.1 fusion.120
  78.6 0.5 broadcast.469
  79.1 0.7 reduce.6
  79.8 0.1 eq.78
  79.9 6.1 %all-to-all-done.1 = f32[16,8,128]{2,1,0:T(8,128)S(1)} async-done(((f32[16,8,128]{2,1,0:T(8,128)}), f32[16,8,128]{2,1,0:T(8,128)S(1)}, u32[]{:S(2)}, u32[]{:S(2)}) %all-to-all-start.1) | async-done | bytes 65568 | tf_op jit(solution)/shard_map/all_to_all | solution.py:799
  86.0 0.1 copy.78
  86.1 0.2 convolution_bitcast_fusion.1
  86.2 0.2 reshape.235
  86.4 8.7 %fusion.26 = f32[1,2,512]{2,1,0:T(2,128)S(1)} fusion(f32[2,1024]{1,0:T(2,128)S(1)} %reshape.235), kind=kOutput, calls=%fused_computation.32 | convolution fusion | flops 19923968 | bytes 12288 | tf_op jit(solution)/shard_map/dot_general | solution.py:809
  95.1 8.8 %fusion.35 = f32[1,2,512]{2,1,0:T(2,128)S(1)} fusion(f32[2,1024]{1,0:T(2,128)S(1)} %reshape.235), kind=kOutput, calls=%fused_computation.35 | convolution fusion | flops 19924992 | bytes 12288 | tf_op jit(solution)/shard_map/dot_general | solution.py:810
  103.9 0.3 copy.81
  104.2 1.3 reshape.267
  105.5 3.5 %all-to-all-start.2 = ((f32[16,1,128]{2,1,0:T(1,128)}), f32[16,1,128]{2,1,0:T(1,128)S(1)}, u32[]{:S(2)}, u32[]{:S(2)}) async-start(f32[16,1,128]{2,1,0:T(1,128)} %reshape.267), calls=%async_computation.2 | async-start | bytes 16384 | tf_op jit(solution)/shard_map/all_to_all | solution.py:821
  109.0 7.2 %all-to-all-done.2 = f32[16,1,128]{2,1,0:T(1,128)S(1)} async-done(((f32[16,1,128]{2,1,0:T(1,128)}), f32[16,1,128]{2,1,0:T(1,128)S(1)}, u32[]{:S(2)}, u32[]{:S(2)}) %all-to-all-start.2) | async-done | bytes 8224 | tf_op jit(solution)/shard_map/all_to_all | solution.py:821
  116.1 0.5 broadcast.471
  116.6 0.7 reduce.7
  117.3 0.8 reshape.268
  118.1 0.3 copy.82
  118.4 0.1 copy.83
  118.4 0.1 reshape.269
  118.5 3.7 %all_to_all.85 = f32[2,1,1024]{2,1,0:T(1,128)S(1)} all-to-all(f32[2,1,1024]{2,1,0:T(1,128)S(1)} %reshape.269), channel_id=1, replica_groups=mesh['grp'=16,'cores'=2] {'cores'}, dimensions={0} | all-to-all | bytes 16384 | tf_op jit(solution)/shard_map/all_to_all | solution.py:820
  122.3 0.7 reduce.8
  122.9 0.1 reshape.270
  123.3 0.6 convolution_bitcast_fusion.2
  123.9 0.1 copy.91
  124.0 0.7 reshape.271
  124.8 3.7 %all-to-all-start.4 = ((f32[16,1,128]{2,1,0:T(1,128)}), f32[16,1,128]{2,1,0:T(1,128)S(1)}, u32[]{:S(2)}, u32[]{:S(2)}) async-start(f32[16,1,128]{2,1,0:T(1,128)} %reshape.271), calls=%async_computation.4 | async-start | bytes 16384 | tf_op jit(solution)/shard_map/all_to_all | solution.py:835
  128.5 7.2 %all-to-all-done.4 = f32[16,1,128]{2,1,0:T(1,128)S(1)} async-done(((f32[16,1,128]{2,1,0:T(1,128)}), f32[16,1,128]{2,1,0:T(1,128)S(1)}, u32[]{:S(2)}, u32[]{:S(2)}) %all-to-all-start.4) | async-done | bytes 8224 | tf_op jit(solution)/shard_map/all_to_all | solution.py:835
  135.6 0.7 reduce.9
  136.3 0.1 reshape.272
  136.5 0.1 reshape.255
  136.6 3.7 %all_to_all.86 = f32[2,4,256]{2,0,1:T(2,128)S(1)} all-to-all(f32[2,4,256]{2,0,1:T(2,128)S(1)} %reshape.255), channel_id=1, replica_groups=mesh['grp'=16,'cores'=2] {'cores'}, dimensions={1} | all-to-all | bytes 16384 | tf_op jit(solution)/shard_map/all_to_all | solution.py:834
  140.3 9.8 %fusion.6 = f32[2,1024]{1,0:T(2,128)S(1)} fusion(s32[512]{0:T(512)S(1)} %fusion.82, f32[2,512]{1,0:T(2,128)S(1)} %bitcast.128, f32[512]{0:T(512)S(1)} %compare_select_fusion.2), kind=kOutput, calls=%fused_computation.13 | convolution fusion | flops 19923968 | bytes 16384 | tf_op jit(solution)/shard_map/dot_general | solution.py:854
  150.2 9.8 %fusion.20 = f32[2,1024]{1,0:T(2,128)S(1)} fusion(f32[2,1024]{1,0:T(2,128)S(1)} %fusion.6, s32[512]{0:T(512)S(1)} %fusion.82, f32[2,512]{1,0:T(2,128)S(1)} %bitcast.127, f32[512]{0:T(512)S(1)} %compare_select_fusion.2), kind=kOutput, calls=%fused_computation.30 | convolution fusion | flops 19926016 | bytes 24576 | tf_op jit(solution)/shard_map/dot_general | solution.py:852
  160.2 0.9 fusion.47
  161.0 3.5 %all-to-all-start.6 = ((f32[16,8,128]{2,1,0:T(8,128)}), f32[16,8,128]{2,1,0:T(8,128)S(1)}, u32[]{:S(2)}, u32[]{:S(2)}) async-start(f32[16,8,128]{2,1,0:T(8,128)} %fusion.47), calls=%async_computation.6 | async-start | bytes 131072 | tf_op jit(solution)/shard_map/all_to_all | solution.py:861
  164.5 7.5 %all-to-all-done.6 = f32[16,8,128]{2,1,0:T(8,128)S(1)} async-done(((f32[16,8,128]{2,1,0:T(8,128)}), f32[16,8,128]{2,1,0:T(8,128)S(1)}, u32[]{:S(2)}, u32[]{:S(2)}) %all-to-all-start.6) | async-done | bytes 65568 | tf_op jit(solution)/shard_map/all_to_all | solution.py:861
  172.0 0.8 fusion.45
  172.9 1.0 copy.108
  (63 shorter events, 1.7 us)
Async XLA Ops:
  3.7 51.8 %all-to-all-start = ((f32[16,1,8]{2,1,0:T(1,128)}), f32[16,1,8]{2,1,0:T(1,128)S(1)}, u32[]{:S(2)}, u32[]{:S(2)}) async-start(f32[16,1,8]{2,1,0:T(1,128)} %bitcast.4), calls=%async_computation | async-start | bytes 16384 | tf_op jit(solution)/shard_map/all_to_all | solution.py:800
  16.1 1.2 copy-start
  17.3 0.7 copy-start.1
  55.5 30.4 %all-to-all-start.1 = ((f32[16,8,128]{2,1,0:T(8,128)}), f32[16,8,128]{2,1,0:T(8,128)S(1)}, u32[]{:S(2)}, u32[]{:S(2)}) async-start(f32[16,8,128]{2,1,0:T(8,128)} %convolution_bitcast_fusion), calls=%async_computation.1 | async-start | bytes 131072 | tf_op jit(solution)/shard_map/all_to_all | solution.py:799
  86.4 8.7 %copy-start.2 = (f32[2,1024]{1,0:T(2,128)}, f32[2,1024]{1,0:T(2,128)S(1)}, u32[]{:S(2)}) copy-start(f32[2,1024]{1,0:T(2,128)S(1)} %reshape.235) | copy-start | bytes 24580
  105.5 10.6 %all-to-all-start.2 = ((f32[16,1,128]{2,1,0:T(1,128)}), f32[16,1,128]{2,1,0:T(1,128)S(1)}, u32[]{:S(2)}, u32[]{:S(2)}) async-start(f32[16,1,128]{2,1,0:T(1,128)} %reshape.267), calls=%async_computation.2 | async-start | bytes 16384 | tf_op jit(solution)/shard_map/all_to_all | solution.py:821
  124.8 10.9 %all-to-all-start.4 = ((f32[16,1,128]{2,1,0:T(1,128)}), f32[16,1,128]{2,1,0:T(1,128)S(1)}, u32[]{:S(2)}, u32[]{:S(2)}) async-start(f32[16,1,128]{2,1,0:T(1,128)} %reshape.271), calls=%async_computation.4 | async-start | bytes 16384 | tf_op jit(solution)/shard_map/all_to_all | solution.py:835
  160.0 13.9 %copy-start.3 = (f32[2,1024]{1,0:T(2,128)}, f32[2,1024]{1,0:T(2,128)S(1)}, u32[]{:S(2)}) copy-start(f32[2,1024]{1,0:T(2,128)S(1)} %fusion.20) | copy-start | bytes 24580
  161.0 11.0 %all-to-all-start.6 = ((f32[16,8,128]{2,1,0:T(8,128)}), f32[16,8,128]{2,1,0:T(8,128)S(1)}, u32[]{:S(2)}, u32[]{:S(2)}) async-start(f32[16,8,128]{2,1,0:T(8,128)} %fusion.47), calls=%async_computation.6 | async-start | bytes 131072 | tf_op jit(solution)/shard_map/all_to_all | solution.py:861

commit v3 on v2

--- a/solution.py
+++ b/solution.py
@@ -3,6 +3,7 @@
 
 import jax
 import jax.numpy as jnp
+import numpy as np
 from jax import lax
 from jax.experimental import pallas as pl
 from jax.experimental.pallas import tpu as pltpu
@@ -295,13 +296,6 @@
     )
 
 
-def fourier_tables(orders):
-    longitudes = jnp.arange(NLON, dtype=jnp.int32)
-    phase_index = longitudes[:, None] * orders[None, :] % NLON
-    angle_rad = phase_index.astype(jnp.float32) * (2.0 * math.pi / NLON)
-    return (jnp.cos(angle_rad), jnp.sin(angle_rad))
-
-
 def legendre_start(sine_lat, orders):
     series_k = jnp.arange(1, DEGREES, dtype=jnp.int32).astype(jnp.float32)
     log_sums = jnp.concatenate(
@@ -384,11 +378,171 @@
     return jnp.concatenate(blocks, axis=0)
 
 
-def solve_spectral(coef_re, coef_im, cosine_lat, sine_lat, weights_lat, orders):
-    pairs = order_pairs(sine_lat, cosine_lat, weights_lat, orders)
-    both = jnp.stack([coef_re.T, coef_im.T], axis=1)
-    synth = jnp.einsum("rcj,rjk->crk", both, pairs, precision=HIGHEST_PRECISION)
-    return (synth[0].T, synth[1].T)
+def exact_dot(left, right, contract):
+    return lax.dot_general(
+        left, right, (contract, ((), ())),
+        precision=HIGHEST_PRECISION, preferred_element_type=jnp.float32,
+    )
+
+
+def wave_constants():
+    order = np.arange(128) // 8
+    used = (np.arange(128) % 8 < 2)[:, None]
+    seg = 2.0 * np.pi / 16 * order[:, None] * np.arange(16)[None, :]
+    turn = 2.0 * np.pi / NLON * order[:, None] * (np.arange(128) % 64)[None, :]
+    high = 2.0 * np.pi / 64 * np.arange(DEGREES // 16)[:, None] * np.arange(64)[None, :]
+    factor = np.full((DEGREES // 16, 128), 2.0)
+    factor[0, :8] = 1.0
+    listed = [np.cos(seg) * used, np.sin(seg) * used, np.cos(turn), np.sin(turn)]
+    listed += [np.cos(high), np.sin(high), factor]
+    return [jnp.asarray(one, jnp.float32) for one in listed]
+
+
+def harmonic_kernel(
+    share, message_ref, pairs_ref, seg_cos, seg_sin, turn_cos, turn_sin, high_cos, high_sin, factor_ref,
+    grid_out, potential_out, home_out,
+    got, coef_send, coef_got, waves, solved, synth_send, synth_got, back_send, home,
+    send_a, recv_a, send_b, recv_b, send_c, recv_c, send_d, recv_d,
+):
+    core_size, groups = lax.axis_size("cores"), lax.axis_size("grp")
+    total = core_size * groups
+    group, core = lax.axis_index("grp"), lax.axis_index("cores")
+    device = group * core_size + core
+    mesh_type = pl.DeviceIdType.MESH
+    barrier = pltpu.get_barrier_semaphore()
+
+    def greet(k, carry):
+        peer = lax.rem(device + k, total)
+        pl.semaphore_signal(
+            barrier, inc=1,
+            device_id=(lax.div(peer, core_size), lax.rem(peer, core_size)), device_id_type=mesh_type,
+        )
+        return carry
+
+    lax.fori_loop(1, total, greet, 0)
+
+    def exchange(source, target, send, recv, over_all, pick):
+        count, me = (total, device) if over_all else (groups, group)
+
+        def copy(k):
+            peer = lax.rem(me + k, count)
+            where = (lax.div(peer, core_size), lax.rem(peer, core_size)) if over_all else (peer, core)
+            return pltpu.make_async_remote_copy(
+                src_ref=source.at[pick(peer)], dst_ref=target.at[me],
+                send_sem=send.at[k], recv_sem=recv.at[k],
+                device_id=where, device_id_type=mesh_type,
+            )
+
+        def begin(k, carry):
+            copy(k).start()
+            return carry
+
+        def finish(k, carry):
+            copy(k).wait_recv()
+            return carry
+
+        def drain(k, carry):
+            copy(k).wait_send()
+            return carry
+
+        lax.fori_loop(1, count, begin, 0)
+        target[me] = source[pick(me)]
+        return lambda: lax.fori_loop(1, count, finish, 0), lambda: lax.fori_loop(1, count, drain, 0)
+
+    same = lambda peer: peer
+    pl.semaphore_wait(barrier, total - 1)
+    arrived, drain_a = exchange(message_ref, got, send_a, recv_a, False, same)
+    capacity = message_ref.shape[1] // 2
+    slots = groups * capacity
+    arrived()
+    rows = got[:, 0:capacity, :].reshape(slots, 128)
+    codes = got[:, capacity : 2 * capacity, :].reshape(slots, 128)
+    seg_ids = lax.broadcasted_iota(jnp.int32, (slots, 128), 1).astype(jnp.float32) + 1.0
+    landing = (codes == seg_ids).astype(jnp.float32)
+    grid = exact_dot(landing, rows, ((0,), (0,)))[0:16]
+    grid_out[...] = grid
+    near_re = exact_dot(seg_cos[...], grid, ((1,), (0,)))
+    near_im = -exact_dot(seg_sin[...], grid, ((1,), (0,)))
+    mid_re = near_re * turn_cos[...] + near_im * turn_sin[...]
+    mid_im = near_im * turn_cos[...] - near_re * turn_sin[...]
+    real_row = lax.broadcasted_iota(jnp.int32, (128, 128), 0) % 8 == 0
+    with_cos = jnp.where(real_row, mid_re, mid_im)
+    with_sin = jnp.where(real_row, mid_im, -mid_re)
+    for z in range(2):
+        lat = slice(64 * z, 64 * z + 64)
+        coef = exact_dot(high_cos[...], with_cos[:, lat], ((1,), (1,)))
+        coef = coef + exact_dot(high_sin[...], with_sin[:, lat], ((1,), (1,)))
+        coef_send[:, z, :] = coef / NLON
+    arrived, drain_b = exchange(
+        coef_send, coef_got, send_b, recv_b, True, lambda peer: lax.div(peer * share, 16)
+    )
+    arrived()
+    cut = jnp.concatenate([coef_got[:, z, :].T for z in range(2)], axis=1)
+    waves[...] = cut.reshape(16, 8, 2 * total)
+    if share < 16:
+        solved[...] = jnp.zeros_like(solved)
+    first = lax.rem(share * device, 16)
+    for order in range(share):
+        solved[first + order] = exact_dot(waves[first + order], pairs_ref[order], ((1,), (0,)))
+    back = solved[...].reshape(128, 2 * total).T
+    for z in range(2):
+        synth_send[:, z, :] = back[z * total : (z + 1) * total]
+    arrived, drain_c = exchange(synth_send, synth_got, send_c, recv_c, True, same)
+    arrived()
+    parts_cos, parts_sin = [], []
+    for z in range(2):
+        part = synth_got[:, z, :]
+        if total > DEGREES // 16:
+            part = jnp.sum(part.reshape(DEGREES // 16, total * 16 // DEGREES, 128), axis=1)
+        part = part * factor_ref[...]
+        parts_cos.append(exact_dot(part, high_cos[...], ((0,), (0,))))
+        parts_sin.append(exact_dot(part, high_sin[...], ((0,), (0,))))
+    full_cos, full_sin = jnp.concatenate(parts_cos, axis=1), jnp.concatenate(parts_sin, axis=1)
+    alpha = full_cos * turn_cos[...] - full_sin * turn_sin[...]
+    beta = full_cos * turn_sin[...] + full_sin * turn_cos[...]
+    potential = exact_dot(seg_cos[...], jnp.where(real_row, alpha, -beta), ((0,), (0,)))
+    potential = potential - exact_dot(seg_sin[...], jnp.where(real_row, beta, alpha), ((0,), (0,)))
+    potential_out[...] = potential
+    spread = exact_dot(landing[:, 0:16], potential, ((1,), (0,)))
+    back_send[...] = spread.reshape(groups, capacity, 128)
+    arrived, drain_d = exchange(back_send, home, send_d, recv_d, False, same)
+    arrived()
+    home_out[...] = home[...]
+    drain_a()
+    drain_b()
+    drain_c()
+    drain_d()
+
+
+def harmonic_solve(message, pairs, total):
+    groups, capacity = message.shape[0], message.shape[1] // 2
+    share = pairs.shape[0]
+    wide = DEGREES // 16
+    vmem = pl.BlockSpec(memory_space=pltpu.VMEM)
+    few, many = pltpu.SemaphoreType.DMA((groups,)), pltpu.SemaphoreType.DMA((total,))
+    room = lambda *shape: pltpu.VMEM(shape, jnp.float32)
+    result = lambda *shape: jax.ShapeDtypeStruct(shape, jnp.float32)
+    return pl.pallas_call(
+        functools.partial(harmonic_kernel, share),
+        out_shape=(result(16, 128), result(16, 128), result(groups, capacity, 128)),
+        in_specs=[vmem] * 9,
+        out_specs=(vmem, vmem, vmem),
+        scratch_shapes=[
+            room(groups, 2 * capacity, 128),
+            room(wide, 8, 128),
+            room(total, 8, 128),
+            room(16, 8, 2 * total),
+            room(16, 8, 2 * total),
+            room(total, 8, 128),
+            room(total, 8, 128),
+            room(groups, capacity, 128),
+            room(groups, capacity, 128),
+            few, few, many, many, many, many, few, few,
+        ],
+        compiler_params=pltpu.CompilerParams(
+            collective_id=1, has_side_effects=True, vmem_limit_bytes=48 * 1024 * 1024
+        ),
+    )(message, pairs, *wave_constants())
 
 
 def body(
@@ -785,7 +939,7 @@
         block_ids[None, :] < block_ids[:, None]
     )
     rank_in_band = jnp.sum(earlier.astype(jnp.int32), axis=1)
-    capacity = max(2, 2 * block_portion // grp_size)
+    capacity = -(-max(2, 2 * block_portion // grp_size) // 8) * 8
     slot_index = band_index * capacity + rank_in_band
     slot_ids = jnp.arange(grp_size * capacity, dtype=jnp.int32)
     placing = (slot_ids[:, None] == slot_index[None, :]).astype(jnp.float32)
@@ -795,70 +949,24 @@
     send_codes = jnp.dot(
         placing, (block_longitude_segment + 1).astype(jnp.float32), precision=HIGHEST_PRECISION
     ).reshape(grp_size, capacity)
-    got_rows, got_codes = (
-        lax.all_to_all(send_rows, "grp", split_axis=0, concat_axis=0, tiled=True),
-        lax.all_to_all(send_codes, "grp", split_axis=0, concat_axis=0, tiled=True),
-    )
-    segments = NLON // 64
-    segment_codes = jnp.arange(1, segments + 1, dtype=jnp.int32).astype(jnp.float32)
-    landing = (got_codes.reshape(-1)[:, None] == segment_codes[None, :]).astype(jnp.float32)
-    gathered = jnp.dot(landing.T, got_rows.reshape(-1, 128), precision=HIGHEST_PRECISION)
-    fac_local = jnp.swapaxes(gathered.reshape(segments, LAT_DEV, 64), 0, 1).reshape(LAT_DEV, NLON)
-    orders_all = jnp.arange(DEGREES, dtype=jnp.int32)
-    cos_table, sin_table = fourier_tables(orders_all)
-    coef_re = jnp.dot(fac_local, cos_table, precision=HIGHEST_PRECISION) / NLON
-    coef_im = -jnp.dot(fac_local, sin_table, precision=HIGHEST_PRECISION) / NLON
+    message = jnp.concatenate(
+        [send_rows, jnp.broadcast_to(send_codes[:, :, None], send_rows.shape)], axis=1
+    )
     lat_total = LAT_DEV * device_total
     degree_share = DEGREES // device_total
-    lat_ids = jnp.arange(lat_total, dtype=jnp.int32)
+    lat_ids = jnp.arange(lat_total, dtype=jnp.int32).reshape(device_total, LAT_DEV).T.reshape(-1)
     colatitude = (lat_ids.astype(jnp.float32) + 0.5) * (math.pi / lat_total)
     cosine_all = jnp.cos(colatitude)
     sine_all = jnp.sin(colatitude)
     weights_all = math.pi / lat_total * sine_all
     own_orders = device * degree_share + jnp.arange(degree_share, dtype=jnp.int32)
-    stacked = jnp.stack([coef_re, coef_im])
-    regrouped = lax.all_to_all(
-        lax.all_to_all(stacked, "grp", split_axis=2, concat_axis=1, tiled=True),
-        "cores",
-        split_axis=2,
-        concat_axis=1,
-        tiled=True,
-    )
-    regrouped = jnp.transpose(
-        regrouped.reshape(2, core_size, grp_size, LAT_DEV, degree_share), (0, 2, 1, 3, 4)
-    ).reshape(2, lat_total, degree_share)
-    synth_re, synth_im = solve_spectral(
-        regrouped[0], regrouped[1], cosine_all, sine_all, weights_all, own_orders
-    )
-    synth_both = jnp.stack([synth_re, synth_im])
-    returned = lax.all_to_all(
-        lax.all_to_all(synth_both, "grp", split_axis=1, concat_axis=2, tiled=True),
-        "cores",
-        split_axis=1,
-        concat_axis=2,
-        tiled=True,
-    )
-    column_ids = jnp.arange(DEGREES, dtype=jnp.int32)
-    order_perm = (
-        degree_share
-        * (
-            core_size * (column_ids // degree_share % grp_size)
-            + column_ids // (grp_size * degree_share)
-        )
-        + column_ids % degree_share
-    )
-    cos_perm, sin_perm = fourier_tables(order_perm)
-    factor = jnp.where(order_perm == 0, jnp.float32(1.0), jnp.float32(2.0))
-    potential_local = jnp.dot(
-        returned[0] * factor, cos_perm.T, precision=HIGHEST_PRECISION
-    ) - jnp.dot(returned[1] * factor, sin_perm.T, precision=HIGHEST_PRECISION)
-    grid_segments = jnp.swapaxes(potential_local.reshape(LAT_DEV, segments, 64), 0, 1).reshape(
-        segments, 128
-    )
-    back_rows = jnp.dot(landing, grid_segments, precision=HIGHEST_PRECISION).reshape(
-        grp_size, capacity, 128
-    )
-    home_rows = lax.all_to_all(back_rows, "grp", split_axis=0, concat_axis=0, tiled=True)
+    pairs = order_pairs(sine_all, cosine_all, weights_all, own_orders)
+    grid_rows, potential_rows, home_rows = harmonic_solve(message, pairs, device_total)
+
+    def by_latitude(found):
+        return jnp.swapaxes(found.reshape(16, LAT_DEV, 64), 0, 1).reshape(LAT_DEV, NLON)
+
+    fac_local, potential_local = by_latitude(grid_rows), by_latitude(potential_rows)
     shell_potential = jnp.dot(placing.T, home_rows.reshape(-1, 128), precision=HIGHEST_PRECISION)
     return (parallel_flow_charge, fac_local, potential_local, shell_potential)
 

time: 175 us -> 98.1 us (0.56)
  Pallas kernels: 34.3 us -> 83.5 us
  starting transfers between devices: 41.9 us -> 0 us
  matrix products: 41.2 us -> 1.14 us
  waiting for transfers between devices: 27.9 us -> 0 us
  blocking collectives: 7.42 us -> 0 us
  other arithmetic: 8.53 us -> 2.43 us
  local copies, waits for them, and re-layouts: 11.6 us -> 9.69 us
    pallas_call x0 -> x1, Pallas kernels: none -> 48.2 us  [harmonic_solve(): pl.pallas_call(functools.partial(harmonic_kernel, share), out_shape=(resu...]
    all_to_all x5 -> x0, starting transfers between devices: 41.9 us -> none  [the longest x1 22.9 us: body(): lax.all_to_all(send_rows, 'grp', split_axis=0, concat_axis=0, tiled=True)]
    dot_general x7 -> x0, matrix products: 38.8 us -> none  [the longest x1 9.83 us: body(): jnp.dot(returned[1] * factor, sin_perm.T, precision=HIGHEST_PRECISION)]
    all_to_all x5 -> x0, waiting for transfers between devices: 27.9 us -> none  [the longest x1 7.5 us: body(): lax.all_to_all(back_rows, 'grp', split_axis=0, concat_axis=0, tiled=True)]
    all_to_all x2 -> x0, blocking collectives: 7.42 us -> none  [the longest x1 3.71 us: body(): lax.all_to_all(lax.all_to_all(synth_both, 'grp', split_axis=1, concat_axi...]
    all_to_all x4 -> x0, other arithmetic: 2.68 us -> none  [the longest x1 0.67 us: body(): lax.all_to_all(lax.all_to_all(stacked, 'grp', split_axis=2, concat_axis=1...]
    all_to_all x11 -> x0, local copies, waits for them, and re-layouts: 2.32 us -> none  [the longest x2 1.27 us: body(): lax.all_to_all(send_codes, 'grp', split_axis=0, concat_axis=0, tiled=True)]
    unnamed x18 -> x29, local copies, waits for them, and re-layouts: 6 us -> 5.46 us
  transfers between devices with their start and end apart: 5 -> 0, of which waited for: 4 -> 0; matrix products, arithmetic and copies ran while one was open for 5% -> 0% of each run, Pallas kernels for 20% -> 0%
where the time goes in v3:
time: 98.1 us; the launch traced here: 97.6 us
  Pallas kernels  83.5 us (85%)
  local copies, waits for them, and re-layouts  9.69 us (10%)
  other arithmetic  2.43 us (2%)
  matrix products  1.14 us (1%)
    pallas_call x1, Pallas kernels, harmonic_solve(): pl.pallas_call(functools.partial(harmonic_kernel, share), out_shape=(resu...  48.2 us
    pallas_call x1, Pallas kernels, advance(): pl.pallas_call(halo_kernel, out_shape=(jax.ShapeDtypeStruct(state_in.shap...  29.4 us
    pallas_call x1, Pallas kernels, order_pairs(): pl.pallas_call(functools.partial(pair_kernel, share_rows), out_shape=jax....  5.9 us
    unnamed x29, local copies, waits for them, and re-layouts  5.46 us

profile of v3, /device:TPU:0, one launch (start us, length us, event | category | flops | bytes accessed | tf_op | source)
XLA Modules:
  0.0 97.6 jit_solution(3875228696365417624)
XLA Ops:
  0.7 0.3 reduce-window.9
  1.0 0.1 slice.32
  1.1 0.1 slice_reduce_fusion
  1.2 0.1 add_bitcast_fusion
  1.3 0.1 pad_maximum_fusion.2
  1.4 0.7 gather_fusion
  2.0 0.1 gather.7
  2.1 0.1 copy.26
  2.2 0.1 add.196
  2.3 0.1 add.197
  2.4 0.1 mul.116
  2.5 0.1 mul.117
  2.6 0.1 fusion.23
  2.6 0.1 reshape.204
  2.7 0.1 mul.120
  2.8 0.1 copy.27
  2.9 0.1 broadcast_bitcast_fusion
  3.0 0.1 reshape.194.order_ref
  3.1 0.1 fusion.20
  3.1 0.1 reshape.203
  3.2 0.1 broadcast_in_dim_tile.10.cosine_ref
  3.3 0.1 reshape.206
  3.4 0.1 broadcast_in_dim_tile.11.weight_ref
  3.5 5.9 %shard_map.166 = f32[8,128,128]{2,1,0:T(8,128)S(1)} custom-call(f32[8,128]{1,0:T(8,128)S(1)} %add_exponential_fusion.start_ref, f32[8,128]{1,0:T(8,128)S(1)} %reshape.194.order_ref, f32[1,128]{1,0:T(1,128)S(1)} %broadcast_in_dim_tile.10.cosine_ref, f32[1,128]{1,0:T(1,128)S(1)} %broadcast_in_dim_tile.11.weight_ref), custom_call_target="tpu_custom_call" | custom-call | tf_op jit(solution)/shard_map/pallas_call | solution.py:889
  9.4 0.1 fusion.30
  9.6 0.7 copy-done.10
  10.4 0.1 pad.14.clone
  10.5 0.1 add_add_fusion.target_ref
  10.6 0.5 copy-done.9
  11.1 0.1 abs_reduce_fusion
  11.2 0.7 fusion.28
  11.8 0.7 copy-done.11
  12.5 0.7 multiply_divide_fusion
  13.1 0.1 broadcast_in_dim_tile.9.rate_ref
  13.2 0.1 mul.102.flux_ref
  13.3 0.6 copy-done.8
  13.9 29.4 %shard_map.165 = (f32[8,64,512]{2,1,0:T(8,128)S(1)}, f32[64,128]{1,0:T(8,128)S(1)}) custom-call(f32[8,64,512]{2,1,0:T(8,128)S(1)} %copy-done, f32[192]{0:T(256)S(1)} %mul.102.flux_ref, f32[3]{0:T(128)S(1)} %broadcast_multiply_fusion.2.speed_ref, f32[8]{0:T(128)S(1)} %copy-done.8, f32[1,128]{1,0:T(1,128)S(1)} %broadcast_in_dim_tile.9.rate_ref, ...), custom_call_target="tpu_custom_call" | custom-call | tf_op jit(solution)/shard_map/pallas_call | solution.py:778
  43.3 0.6 copy-done.12
  43.9 0.2 convert_reduce_fusion
  44.1 0.2 convolution_bitcast_fusion
  44.3 0.5 copy-done.13
  44.8 0.1 convolution_bitcast_fusion.1
  44.9 0.1 broadcast_in_dim.36
  45.0 0.0 copy-start.5
  45.1 0.0 copy-start.6
  45.1 0.0 copy-start.7
  45.1 0.1 broadcast_in_dim.37
  45.2 0.0 copy-start.2
  45.2 0.0 copy-start.3
  45.2 0.0 copy-start.4
  45.2 0.6 copy-done.5
  45.8 0.0 copy-done.6
  45.8 0.0 copy-done.7
  45.8 0.2 copy-done.1
  46.0 0.0 copy-done.2
  46.1 0.0 copy-done.3
  46.1 0.0 copy-done.4
  46.1 48.2 %shard_map.167 = (f32[16,128]{1,0:T(8,128)S(1)}, f32[16,128]{1,0:T(8,128)S(1)}, f32[16,8,128]{2,1,0:T(8,128)S(1)}) custom-call(f32[16,16,128]{2,1,0:T(8,128)S(1)} %pad_maximum_fusion.1.message_ref, f32[16,64,64]{2,1,0:T(8,128)S(1)} %pad_maximum_fusion.pairs_ref, f32[128,16]{1,0:T(8,128)S(1)} %copy-done.1, f32[128,16]{1,0:T(8,128)S(1)} %copy-done.2, ...), custom_call_target="tpu_custom_call" | custom-call | tf_op jit(solution)/shard_map/pallas_call | solution.py:525
  94.3 0.9 fusion
  95.1 0.1 reshape.195
  95.2 0.7 reshape.196
  95.9 0.1 reshape.197
  96.0 0.7 reshape.198
  96.7 1.0 copy.31
  (35 shorter events, 0.3 us)
Async XLA Ops:
  9.4 3.9 %copy-start = (f32[8,64,512]{2,1,0:T(8,128)S(1)}, f32[8,64,512]{2,1,0:T(8,128)}, u32[]{:S(2)}) copy-start(f32[8,64,512]{2,1,0:T(8,128)} %state_ref.1) | copy-start | bytes 3145732
  9.6 0.8 copy-start.10
  10.4 0.7 copy-start.9
  11.8 0.7 copy-start.11
  13.2 0.7 copy-start.8
  43.3 0.7 copy-start.12
  44.1 0.7 copy-start.13
  45.0 0.7 copy-start.5
  45.1 0.7 copy-start.6
  45.1 0.7 copy-start.7
  45.2 0.9 copy-start.1
  45.2 0.9 copy-start.2
  45.2 0.9 copy-start.3
  45.2 0.9 copy-start.4

commit v4 on v3

--- a/solution.py
+++ b/solution.py
@@ -36,8 +36,9 @@
 
 def halo_kernel(
     state_ref, flux_ref, speed_ref, coef_ref, rate_ref, target_ref,
-    state_out, patch_out,
-    cells, diffs, laps, change, own, before, after, picks,
+    start_ref, order_ref, cosine_ref, weight_ref,
+    state_out, patch_out, pairs_out,
+    table, cells, diffs, laps, change, own, before, after, picks,
     send_prev, send_next, recv_prev, recv_next,
 ):
     variables, blocks = state_ref.shape[0], state_ref.shape[1]
@@ -216,6 +217,9 @@
             for face in range(5):
                 hit = row_ids == target_ref[face : face + 1, :]
                 picks[face] = hit.astype(jnp.float32).astype(jnp.bfloat16)
+            pair_kernel(
+                pairs_out.shape[0], start_ref, order_ref, cosine_ref, weight_ref, pairs_out, table
+            )
         for direction in range(3):
             arrive(step, direction)
             sides(step, direction)
@@ -241,7 +245,7 @@
             left(step, direction)
 
 
-def advance(state_in, flux_derivative_matrices, speeds, rate_block, local_index, parallel_flow_coefficients):
+def advance(state_in, flux_derivative_matrices, speeds, rate_block, local_index, parallel_flow_coefficients, terms, share_rows):
     variables, blocks = state_in.shape[0], state_in.shape[1]
     lanes = 2 * blocks
     here = jnp.where(
@@ -258,6 +262,7 @@
     )
     rate = jnp.tile(rate_block, 2)[None, :]
     vmem, smem = pl.BlockSpec(memory_space=pltpu.VMEM), pl.BlockSpec(memory_space=pltpu.SMEM)
+    width = terms[0].shape[1]
     whole = (variables, 256, lanes)
     faces = (STEPS, 3, 64 * variables, lanes)
     pairs = pltpu.SemaphoreType.DMA((STEPS, 3))
@@ -266,10 +271,12 @@
         out_shape=(
             jax.ShapeDtypeStruct(state_in.shape, jnp.float32),
             jax.ShapeDtypeStruct((blocks, 128), jnp.float32),
+            jax.ShapeDtypeStruct((share_rows, width, width), jnp.float32),
         ),
-        in_specs=[vmem, smem, smem, smem, vmem, vmem],
-        out_specs=(vmem, vmem),
+        in_specs=[vmem, smem, smem, smem, vmem, vmem] + [vmem] * 4,
+        out_specs=(vmem, vmem, vmem),
         scratch_shapes=[
+            pltpu.VMEM((width // 128, DEGREES * terms[0].shape[0], 128), jnp.float32),
             pltpu.VMEM(whole, jnp.float32),
             pltpu.VMEM(whole, jnp.float32),
             pltpu.VMEM(whole, jnp.float32),
@@ -293,6 +300,7 @@
         parallel_flow_coefficients,
         rate,
         target,
+        *terms,
     )
 
 
@@ -350,7 +358,7 @@
         )
 
 
-def order_pairs(sine_lat, cosine_lat, weights_lat, orders):
+def order_terms(sine_lat, cosine_lat, weights_lat, orders):
     lat_total, share = sine_lat.shape[0], orders.shape[0]
     side = max(1, min(share, 128 // lat_total))
     share_rows, lanes = share // side, side * lat_total
@@ -365,12 +373,11 @@
     order_real = jnp.pad(order_real, ((0, height - share_rows), (0, 0)))
     cosine = jnp.tile(cosine_lat, side)[None, :]
     weight = jnp.tile(weights_lat, side)[None, :]
-    pairs = pl.pallas_call(
-        functools.partial(pair_kernel, share_rows),
-        out_shape=jax.ShapeDtypeStruct((share_rows, lanes, lanes), jnp.float32),
-        scratch_shapes=[pltpu.VMEM((lanes // 128, DEGREES * height, 128), jnp.float32)],
-        compiler_params=pltpu.CompilerParams(vmem_limit_bytes=48 * 1024 * 1024),
-    )(start, order_real, cosine, weight)
+    return start, order_real, cosine, weight
+
+
+def order_blocks(pairs, lat_total, share):
+    side = share // pairs.shape[0]
     blocks = [
         pairs[:, lat_total * at : lat_total * (at + 1), lat_total * at : lat_total * (at + 1)]
         for at in range(side)
@@ -529,12 +536,12 @@
         out_specs=(vmem, vmem, vmem),
         scratch_shapes=[
             room(groups, 2 * capacity, 128),
-            room(wide, 8, 128),
-            room(total, 8, 128),
+            room(wide, 2, 128),
+            room(total, 2, 128),
             room(16, 8, 2 * total),
             room(16, 8, 2 * total),
-            room(total, 8, 128),
-            room(total, 8, 128),
+            room(total, 2, 128),
+            room(total, 2, 128),
             room(groups, capacity, 128),
             room(groups, capacity, 128),
             few, few, many, many, many, many, few, few,
@@ -543,367 +550,6 @@
             collective_id=1, has_side_effects=True, vmem_limit_bytes=48 * 1024 * 1024
         ),
     )(message, pairs, *wave_constants())
-
-
-def body(
-    invariant_fluid_quantities,
-    flux_derivative_matrices,
-    levels,
-    neighbours,
-    block_latitude_band,
-    block_longitude_segment,
-    parallel_flow_coefficients,
-):
-    grp_size = lax.axis_size("grp")
-    core_size = lax.axis_size("cores")
-    device_total = grp_size * core_size
-    block_portion = invariant_fluid_quantities.shape[1]
-    device = lax.axis_index("grp") * core_size + lax.axis_index("cores")
-    has_prev, has_next = device > 0, device < total - 1
-    prev_id = (lax.div(device - 1, core_size), lax.rem(device - 1 + core_size, core_size))
-    next_id = (lax.div(device + 1, core_size), lax.rem(device + 1, core_size))
-    mesh_type = pl.DeviceIdType.MESH
-    barrier = pltpu.get_barrier_semaphore()
-
-    @pl.when(has_prev)
-    def _():
-        pl.semaphore_signal(barrier, inc=1, device_id=prev_id, device_id_type=mesh_type)
-
-    @pl.when(has_next)
-    def _():
-        pl.semaphore_signal(barrier, inc=1, device_id=next_id, device_id_type=mesh_type)
-
-    @pl.when(jnp.logical_not(has_prev))
-    def _():
-        before[...] = jnp.zeros_like(before)
-
-    @pl.when(jnp.logical_not(has_next))
-    def _():
-        after[...] = jnp.zeros_like(after)
-
-    left_half = lax.broadcasted_iota(jnp.int32, (1, lanes), 1) < blocks
-    for v in range(variables):
-        both = jnp.concatenate([state_ref[v, :, 0:256], state_ref[v, :, 256:512]], axis=0)
-        cells[v] = both.T
-
-    def copies(step, direction):
-        to_prev = pltpu.make_async_remote_copy(
-            src_ref=own.at[step, direction], dst_ref=after.at[step, direction],
-            send_sem=send_prev.at[step, direction], recv_sem=recv_next.at[step, direction],
-            device_id=prev_id, device_id_type=mesh_type,
-        )
-        to_next = pltpu.make_async_remote_copy(
-            src_ref=own.at[step, direction], dst_ref=before.at[step, direction],
-            send_sem=send_next.at[step, direction], recv_sem=recv_prev.at[step, direction],
-            device_id=next_id, device_id_type=mesh_type,
-        )
-        return to_prev, to_next
-
-    def start(step, direction):
-        to_prev, to_next = copies(step, direction)
-
-        @pl.when(has_prev)
-        def _():
-            to_prev.start()
-
-        @pl.when(has_next)
-        def _():
-            to_next.start()
-
-    def arrive(step, direction):
-        to_prev, to_next = copies(step, direction)
-
-        @pl.when(has_prev)
-        def _():
-            to_next.wait_recv()
-
-        @pl.when(has_next)
-        def _():
-            to_prev.wait_recv()
-
-    def left(step, direction):
-        to_prev, to_next = copies(step, direction)
-
-        @pl.when(has_prev)
-        def _():
-            to_prev.wait_send()
-
-        @pl.when(has_next)
-        def _():
-            to_next.wait_send()
-
-    def fill(step, direction):
-        for v in range(variables):
-            if direction == 0:
-                own[step, 0, pl.ds(64 * v, 64), :] = jnp.where(
-                    left_half, cells[v, 0:64, :], cells[v, 192:256, :]
-                )
-            elif direction == 1:
-                for side in range(2):
-                    for x in range(4):
-                        own[step, 1, pl.ds(256 * side + 32 * v + 8 * x, 8), :] = cells[
-                            v, pl.ds(64 * x + 56 * side, 8), :
-                        ]
-            else:
-                for side in range(2):
-                    own[step, 2, pl.ds(256 * side + 32 * v, 32), :] = cells[
-                        v, pl.ds(7 * side, 32, stride=8), :
-                    ]
-
-    def gathered(step, direction, first, rows, face):
-        part = pl.ds(first, rows)
-        table = jnp.concatenate(
-            [before[step, direction, part, :], own[step, direction, part, :], after[step, direction, part, :]],
-            axis=1,
-        )
-        return split_dot(table, picks[face])
-
-    def keep(v, at, rows, lower, upper, here):
-        diffs[v, pl.ds(at, rows), :] = upper - lower
-        laps[v, pl.ds(at, rows), :] = upper - 2.0 * here + lower
-
-    def sides(step, direction):
-        if direction == 0:
-            known = target_ref[0:1, :] >= 0
-            ghosts = gathered(step, 0, 0, 64 * variables, 0)
-            for v in range(variables):
-                ghost = jnp.where(known, ghosts[64 * v : 64 * v + 64], own[step, 0, pl.ds(64 * v, 64), :])
-                slabs = [cells[v, pl.ds(64 * x, 64), :] for x in range(4)]
-                first = jnp.where(left_half, ghost, pltpu.roll(slabs[3], blocks, 1))
-                last = jnp.where(left_half, pltpu.roll(slabs[0], blocks, 1), ghost)
-                line = [first] + slabs + [last]
-                for x in range(4):
-                    keep(v, 64 * x, 64, line[x], line[x + 2], slabs[x])
-            return
-        near, far = 2 * direction - 1, 2 * direction
-        rows = 32 * variables
-        low = gathered(step, direction, rows, rows, near)
-        high = gathered(step, direction, 0, rows, far)
-        know_low, know_high = target_ref[near : near + 1, :] >= 0, target_ref[far : far + 1, :] >= 0
-        for v in range(variables):
-            part = slice(32 * v, 32 * v + 32)
-            low_v = jnp.where(know_low, low[part], own[step, direction, pl.ds(32 * v, 32), :])
-            high_v = jnp.where(know_high, high[part], own[step, direction, pl.ds(rows + 32 * v, 32), :])
-            if direction == 1:
-                for x in range(4):
-                    slab = cells[v, pl.ds(64 * x, 64), :]
-                    lower = jnp.concatenate([low_v[8 * x : 8 * x + 8], slab[0:56]], axis=0)
-                    upper = jnp.concatenate([slab[8:64], high_v[8 * x : 8 * x + 8]], axis=0)
-                    keep(v, 64 * x, 64, lower, upper, slab)
-            else:
-                whole = cells[v].reshape(32, 8, lanes)
-                height = lax.broadcasted_iota(jnp.int32, (32, 8, lanes), 1)
-                lower = jnp.where(height == 0, low_v[:, None, :], pltpu.roll(whole, 1, 1))
-                upper = jnp.where(height == 7, high_v[:, None, :], pltpu.roll(whole, 7, 1))
-                keep(v, 0, 256, lower.reshape(256, lanes), upper.reshape(256, lanes), cells[v])
-
-    def mix(direction, final):
-        rows = 16
-
-        def one_chunk(chunk, carry):
-            part = pl.ds(pl.multiple_of(chunk * rows, rows), rows)
-            steps = [diffs[v, part, :] for v in range(variables)]
-            for i in range(variables):
-                total_i = -speed_ref[direction] * laps[i, part, :]
-                for j in range(variables):
-                    total_i = total_i + flux_ref[(direction * variables + i) * variables + j] * steps[j]
-                if direction > 0:
-                    total_i = total_i + change[i, part, :]
-                if final:
-                    cells[i, part, :] = cells[i, part, :] - rate_ref[0:1, :] * total_i
-                else:
-                    change[i, part, :] = total_i
-            return carry
-
-        lax.fori_loop(0, 256 // rows, one_chunk, 0)
-
-    fill(0, 0)
-
-    pl.semaphore_wait(barrier, has_prev.astype(jnp.int32) + has_next.astype(jnp.int32))
-    for step in range(STEPS):
-        for direction in range(3):
-            if step > 0 or direction > 0:
-                fill(step, direction)
-            start(step, direction)
-        if step == 0:
-            row_ids = lax.broadcasted_iota(jnp.int32, (3 * lanes, lanes), 0)
-            for face in range(5):
-                hit = row_ids == target_ref[face : face + 1, :]
-                picks[face] = hit.astype(jnp.float32).astype(jnp.bfloat16)
-        for direction in range(3):
-            arrive(step, direction)
-            sides(step, direction)
-            mix(direction, direction == 2)
-    for v in range(variables):
-        flat = cells[v].T
-        state_out[v, :, 0:256] = flat[0:blocks]
-        state_out[v, :, 256:512] = flat[blocks:lanes]
-    layers = []
-    for z in range(2):
-        layer = coef_ref[0] * cells[0, pl.ds(z, 32, stride=8), :]
-        for v in range(1, variables):
-            layer = layer + coef_ref[v] * cells[v, pl.ds(z, 32, stride=8), :]
-        layers.append(layer)
-    turned = jnp.concatenate(layers + layers, axis=0).T
-    for z in range(2):
-        for half in range(2):
-            patch_out[:, pl.ds(64 * z + 32 * half, 32)] = turned[
-                blocks * half : blocks * half + blocks, 32 * z : 32 * z + 32
-            ]
-    for step in range(STEPS):
-        for direction in range(3):
-            left(step, direction)
-
-
-def advance(state_in, flux_derivative_matrices, speeds, rate_block, local_index, parallel_flow_coefficients):
-    variables, blocks = state_in.shape[0], state_in.shape[1]
-    lanes = 2 * blocks
-    here = jnp.where(
-        local_index >= 0, local_index // blocks * lanes + local_index % blocks, -1
-    ).T
-    right = jnp.where(here >= 0, here + blocks, -1)
-    target = jnp.concatenate(
-        [
-            jnp.concatenate([right[0:1], here[1:2]], axis=1),
-            jnp.concatenate([here[2:6], right[2:6]], axis=1),
-            jnp.full((3, lanes), -1, jnp.int32),
-        ],
-        axis=0,
-    )
-    rate = jnp.tile(rate_block, 2)[None, :]
-    vmem, smem = pl.BlockSpec(memory_space=pltpu.VMEM), pl.BlockSpec(memory_space=pltpu.SMEM)
-    whole = (variables, 256, lanes)
-    faces = (STEPS, 3, 64 * variables, lanes)
-    pairs = pltpu.SemaphoreType.DMA((STEPS, 3))
-    return pl.pallas_call(
-        halo_kernel,
-        out_shape=(
-            jax.ShapeDtypeStruct(state_in.shape, jnp.float32),
-            jax.ShapeDtypeStruct((blocks, 128), jnp.float32),
-        ),
-        in_specs=[vmem, smem, smem, smem, vmem, vmem],
-        out_specs=(vmem, vmem),
-        scratch_shapes=[
-            pltpu.VMEM(whole, jnp.float32),
-            pltpu.VMEM(whole, jnp.float32),
-            pltpu.VMEM(whole, jnp.float32),
-            pltpu.VMEM(whole, jnp.float32),
-            pltpu.VMEM(faces, jnp.float32),
-            pltpu.VMEM(faces, jnp.float32),
-            pltpu.VMEM(faces, jnp.float32),
-            pltpu.VMEM((5, 3 * lanes, lanes), jnp.bfloat16),
-            pairs,
-            pairs,
-            pairs,
-            pairs,
-        ],
-        compiler_params=pltpu.CompilerParams(
-            collective_id=0, has_side_effects=True, vmem_limit_bytes=48 * 1024 * 1024
-        ),
-    )(
-        state_in,
-        0.5 * flux_derivative_matrices.reshape(-1),
-        0.5 * speeds,
-        parallel_flow_coefficients,
-        rate,
-        target,
-    )
-
-
-def fourier_tables(orders):
-    longitudes = jnp.arange(NLON, dtype=jnp.int32)
-    phase_index = longitudes[:, None] * orders[None, :] % NLON
-    angle_rad = phase_index.astype(jnp.float32) * (2.0 * math.pi / NLON)
-    return (jnp.cos(angle_rad), jnp.sin(angle_rad))
-
-
-def legendre_start(sine_lat, orders):
-    series_k = jnp.arange(1, DEGREES, dtype=jnp.int32).astype(jnp.float32)
-    log_sums = jnp.concatenate(
-        [
-            jnp.zeros((1,), jnp.float32),
-            jnp.cumsum(0.5 * jnp.log((2.0 * series_k + 1.0) / (2.0 * series_k))),
-        ]
-    )
-    log_base = jnp.take(log_sums, orders)
-    order_real = orders.astype(jnp.float32)
-    return jnp.exp(
-        0.5 * math.log(0.5) + log_base[None, :] + order_real[None, :] * jnp.log(sine_lat)[:, None]
-    )
-
-
-def pair_kernel(share_rows, start_ref, order_ref, cosine_ref, weight_ref, out_ref, table):
-    diagonal = start_ref[...]
-    height, pieces = diagonal.shape[0], diagonal.shape[1] // 128
-    order = order_ref[...]
-    square = order * order
-    cosine = cosine_ref[...]
-
-    def one_degree(degree, carried):
-        previous, before = carried
-        real = degree.astype(jnp.float32)
-        top = jnp.full(diagonal.shape, 4.0 * real * real - 1.0, jnp.float32)
-        lower = real - 1.0
-        low = jnp.full(diagonal.shape, 4.0 * lower * lower - 1.0, jnp.float32)
-        up = jnp.sqrt(jnp.maximum(top, 1.0) / jnp.maximum(real * real - square, 1.0))
-        back = jnp.sqrt(jnp.maximum(lower * lower - square, 0.0) / jnp.maximum(low, 1.0))
-        present = (up * cosine) * previous + (-up * back) * before
-        present = present + jnp.where(order == real, diagonal, 0.0)
-        at = pl.multiple_of(degree * height, height)
-        for piece in range(pieces):
-            table[piece, pl.ds(at, height), :] = present[:, 128 * piece : 128 * (piece + 1)]
-        return present, previous
-
-    zero = diagonal * 0.0
-    lax.fori_loop(0, DEGREES, one_degree, (zero, zero), unroll=8)
-    degrees = lax.broadcasted_iota(jnp.int32, (DEGREES, 1), 0).astype(jnp.float32)
-    gain = POT_GAIN / (degrees * (degrees + 1.0) + KAPPA2)
-    for row in range(share_rows):
-        rows = jnp.concatenate(
-            [table[piece, pl.ds(row, DEGREES, stride=height), :] for piece in range(pieces)], axis=1
-        )
-        out_ref[row] = lax.dot_general(
-            rows * weight_ref[...],
-            rows * gain,
-            (((0,), (0,)), ((), ())),
-            precision=HIGHEST_PRECISION,
-            preferred_element_type=jnp.float32,
-        )
-
-
-def order_pairs(sine_lat, cosine_lat, weights_lat, orders):
-    lat_total, share = sine_lat.shape[0], orders.shape[0]
-    side = max(1, min(share, 128 // lat_total))
-    share_rows, lanes = share // side, side * lat_total
-    start = legendre_start(sine_lat, orders).T.reshape(side, share_rows, lat_total)
-    start = jnp.swapaxes(start, 0, 1).reshape(share_rows, lanes)
-    order_real = jnp.broadcast_to(
-        orders.astype(jnp.float32).reshape(side, share_rows, 1), (side, share_rows, lat_total)
-    )
-    order_real = jnp.swapaxes(order_real, 0, 1).reshape(share_rows, lanes)
-    height = -(-share_rows // 8) * 8
-    start = jnp.pad(start, ((0, height - share_rows), (0, 0)))
-    order_real = jnp.pad(order_real, ((0, height - share_rows), (0, 0)))
-    cosine = jnp.tile(cosine_lat, side)[None, :]
-    weight = jnp.tile(weights_lat, side)[None, :]
-    pairs = pl.pallas_call(
-        functools.partial(pair_kernel, share_rows),
-        out_shape=jax.ShapeDtypeStruct((share_rows, lanes, lanes), jnp.float32),
-        scratch_shapes=[pltpu.VMEM((lanes // 128, DEGREES * height, 128), jnp.float32)],
-        compiler_params=pltpu.CompilerParams(vmem_limit_bytes=48 * 1024 * 1024),
-    )(start, order_real, cosine, weight)
-    blocks = [
-        pairs[:, lat_total * at : lat_total * (at + 1), lat_total * at : lat_total * (at + 1)]
-        for at in range(side)
-    ]
-    return jnp.concatenate(blocks, axis=0)
-
-
-def solve_spectral(coef_re, coef_im, cosine_lat, sine_lat, weights_lat, orders):
-    pairs = order_pairs(sine_lat, cosine_lat, weights_lat, orders)
-    both = jnp.stack([coef_re.T, coef_im.T], axis=1)
-    synth = jnp.einsum("rcj,rjk->crk", both, pairs, precision=HIGHEST_PRECISION)
-    return (synth[0].T, synth[1].T)
 
 
 def body(
@@ -925,33 +571,6 @@
     rate_block = COURANT * jnp.exp2(levels.astype(jnp.float32) - (LEVELS - 1)) / jnp.max(speeds)
     offset = (device - 1) * block_portion
     local_index = jnp.where(neighbours >= 0, neighbours - offset, -1)
-    parallel_flow_charge, patches = advance(
-        invariant_fluid_quantities,
-        flux_derivative_matrices,
-        speeds,
-        rate_block,
-        local_index,
-        parallel_flow_coefficients,
-    )
-    band_index = block_latitude_band[:, 0]
-    block_ids = jnp.arange(block_portion, dtype=jnp.int32)
-    earlier = (band_index[None, :] == band_index[:, None]) & (
-        block_ids[None, :] < block_ids[:, None]
-    )
-    rank_in_band = jnp.sum(earlier.astype(jnp.int32), axis=1)
-    capacity = -(-max(2, 2 * block_portion // grp_size) // 8) * 8
-    slot_index = band_index * capacity + rank_in_band
-    slot_ids = jnp.arange(grp_size * capacity, dtype=jnp.int32)
-    placing = (slot_ids[:, None] == slot_index[None, :]).astype(jnp.float32)
-    send_rows = jnp.dot(placing, patches, precision=HIGHEST_PRECISION).reshape(
-        grp_size, capacity, 128
-    )
-    send_codes = jnp.dot(
-        placing, (block_longitude_segment + 1).astype(jnp.float32), precision=HIGHEST_PRECISION
-    ).reshape(grp_size, capacity)
-    message = jnp.concatenate(
-        [send_rows, jnp.broadcast_to(send_codes[:, :, None], send_rows.shape)], axis=1
-    )
     lat_total = LAT_DEV * device_total
     degree_share = DEGREES // device_total
     lat_ids = jnp.arange(lat_total, dtype=jnp.int32).reshape(device_total, LAT_DEV).T.reshape(-1)
@@ -960,7 +579,38 @@
     sine_all = jnp.sin(colatitude)
     weights_all = math.pi / lat_total * sine_all
     own_orders = device * degree_share + jnp.arange(degree_share, dtype=jnp.int32)
-    pairs = order_pairs(sine_all, cosine_all, weights_all, own_orders)
+    terms = order_terms(sine_all, cosine_all, weights_all, own_orders)
+    share_rows = degree_share * lat_total // terms[0].shape[1]
+    parallel_flow_charge, patches, pairs = advance(
+        invariant_fluid_quantities,
+        flux_derivative_matrices,
+        speeds,
+        rate_block,
+        local_index,
+        parallel_flow_coefficients,
+        terms,
+        share_rows,
+    )
+    band_index = block_latitude_band[:, 0]
+    block_ids = jnp.arange(block_portion, dtype=jnp.int32)
+    earlier = (band_index[None, :] == band_index[:, None]) & (
+        block_ids[None, :] < block_ids[:, None]
+    )
+    rank_in_band = jnp.sum(earlier.astype(jnp.int32), axis=1)
+    capacity = -(-max(2, 2 * block_portion // grp_size) // 8) * 8
+    slot_index = band_index * capacity + rank_in_band
+    slot_ids = jnp.arange(grp_size * capacity, dtype=jnp.int32)
+    placing = (slot_ids[:, None] == slot_index[None, :]).astype(jnp.float32)
+    send_rows = jnp.dot(placing, patches, precision=HIGHEST_PRECISION).reshape(
+        grp_size, capacity, 128
+    )
+    send_codes = jnp.dot(
+        placing, (block_longitude_segment + 1).astype(jnp.float32), precision=HIGHEST_PRECISION
+    ).reshape(grp_size, capacity)
+    message = jnp.concatenate(
+        [send_rows, jnp.broadcast_to(send_codes[:, :, None], send_rows.shape)], axis=1
+    )
+    pairs = order_blocks(pairs, lat_total, degree_share)
     grid_rows, potential_rows, home_rows = harmonic_solve(message, pairs, device_total)
 
     def by_latitude(found):

time: 98.1 us -> 92 us (0.938)
  Pallas kernels: 83.5 us -> 76.3 us
  local copies, waits for them, and re-layouts: 9.69 us -> 11 us
    pallas_call x1 -> x0, Pallas kernels: 5.9 us -> none  [order_pairs(): pl.pallas_call(functools.partial(pair_kernel, share_rows), out_shape=jax....]
    pallas_call x1, Pallas kernels: 48.2 us -> 46.8 us  [harmonic_solve(): pl.pallas_call(functools.partial(harmonic_kernel, share), out_shape=(resu...]
    unnamed x29, local copies, waits for them, and re-layouts: 5.46 us -> 6.73 us
where the time goes in v4:
time: 92 us; the launch traced here: 91.7 us
  Pallas kernels  76.3 us (83%)
  local copies, waits for them, and re-layouts  11 us (12%)
  other arithmetic  2.42 us (3%)
  matrix products  1.14 us (1%)
    pallas_call x1, Pallas kernels, harmonic_solve(): pl.pallas_call(functools.partial(harmonic_kernel, share), out_shape=(resu...  46.8 us
    pallas_call x1, Pallas kernels, advance(): pl.pallas_call(halo_kernel, out_shape=(jax.ShapeDtypeStruct(state_in.shap...  29.4 us
    unnamed x29, local copies, waits for them, and re-layouts  6.73 us

profile of v4, /device:TPU:0, one launch (start us, length us, event | category | flops | bytes accessed | tf_op | source)
XLA Modules:
  0.0 91.7 jit_solution(14651654391283198305)
XLA Ops:
  0.7 0.3 reduce-window.9
  1.0 0.1 slice.32
  1.1 0.1 slice_reduce_fusion
  1.2 0.1 add_bitcast_fusion
  1.3 0.1 pad_maximum_fusion.2
  1.4 0.7 gather_fusion
  2.0 0.1 gather.7
  2.1 0.1 copy.26
  2.2 0.1 add.193
  2.3 0.1 add.194
  2.4 0.1 mul.114
  2.5 0.1 mul.115
  2.6 0.1 fusion.25
  2.6 0.1 reshape.204
  2.7 0.1 mul.118
  2.8 0.7 copy-done.10
  3.6 0.1 pad.14.clone
  3.6 0.1 add_add_fusion.target_ref
  3.7 0.1 copy.27
  3.8 0.1 broadcast_bitcast_fusion
  3.9 0.1 reshape.193.order_ref
  4.0 0.6 copy-done.9
  4.5 0.1 abs_reduce_fusion
  4.6 0.7 fusion.28
  5.3 0.7 copy-done.11
  5.9 0.7 multiply_divide_fusion
  6.6 0.1 broadcast_in_dim_tile.9.rate_ref
  6.7 0.1 mul.102.flux_ref
  6.8 0.1 reshape.203
  6.9 0.1 broadcast_in_dim_tile.10.cosine_ref
  7.0 0.1 reshape.206
  7.1 0.1 broadcast_in_dim_tile.11.weight_ref
  7.2 0.6 copy-done.8
  7.8 1.2 %copy-done = f32[8,64,512]{2,1,0:T(8,128)S(1)} copy-done((f32[8,64,512]{2,1,0:T(8,128)S(1)}, f32[8,64,512]{2,1,0:T(8,128)}, u32[]{:S(2)}) %copy-start) | copy-done | bytes 1048600
  9.0 29.4 %shard_map.165 = (f32[8,64,512]{2,1,0:T(8,128)S(1)}, f32[64,128]{1,0:T(8,128)S(1)}, f32[8,128,128]{2,1,0:T(8,128)S(1)}) custom-call(f32[8,64,512]{2,1,0:T(8,128)S(1)} %copy-done, f32[192]{0:T(256)S(1)} %mul.102.flux_ref, f32[3]{0:T(128)S(1)} %broadcast_multiply_fusion.2.speed_ref, f32[8]{0:T(128)S(1)} %copy-done.8, ...), custom_call_target="tpu_custom_call" | custom-call | tf_op jit(solution)/shard_map/pallas_call | solution.py:269
  38.4 0.1 fusion.30
  38.6 0.0 copy-start.12
  38.6 0.6 copy-done.12
  39.3 0.2 convert_reduce_fusion
  39.5 0.2 convolution_bitcast_fusion
  39.6 0.5 copy-done.13
  40.1 0.1 convolution_bitcast_fusion.1
  40.2 0.1 broadcast_in_dim.37
  40.4 0.0 copy-start.5
  40.4 0.0 copy-start.6
  40.4 0.0 copy-start.7
  40.4 0.1 broadcast_in_dim.38
  40.5 0.0 copy-start.2
  40.5 0.0 copy-start.3
  40.5 0.0 copy-start.4
  40.6 0.6 copy-done.5
  41.1 0.0 copy-done.6
  41.1 0.0 copy-done.7
  41.2 0.2 copy-done.1
  41.4 0.0 copy-done.2
  41.4 0.0 copy-done.3
  41.4 0.0 copy-done.4
  41.5 46.8 %shard_map.166 = (f32[16,128]{1,0:T(8,128)S(1)}, f32[16,128]{1,0:T(8,128)S(1)}, f32[16,8,128]{2,1,0:T(8,128)S(1)}) custom-call(f32[16,16,128]{2,1,0:T(8,128)S(1)} %pad_maximum_fusion.1.message_ref, f32[16,64,64]{2,1,0:T(8,128)S(1)} %pad_maximum_fusion.pairs_ref, f32[128,16]{1,0:T(8,128)S(1)} %copy-done.1, f32[128,16]{1,0:T(8,128)S(1)} %copy-done.2, ...), custom_call_target="tpu_custom_call" | custom-call | tf_op jit(solution)/shard_map/pallas_call | solution.py:532
  88.3 0.1 reshape.195
  88.4 0.7 reshape.196
  89.1 0.1 reshape.197
  89.2 0.7 reshape.198
  89.8 0.8 fusion
  90.7 1.0 %copy.31 = f32[8,64,512]{2,1,0:T(8,128)} copy(f32[8,64,512]{2,1,0:T(8,128)S(1)} %get-tuple-element.28) | data formatting | bytes 2097152
  (34 shorter events, 0.3 us)
Async XLA Ops:
  2.8 0.7 copy-start.10
  3.8 0.7 copy-start.9
  5.3 0.7 copy-start.11
  7.1 0.7 copy-start.8
  7.8 1.2 %copy-start = (f32[8,64,512]{2,1,0:T(8,128)S(1)}, f32[8,64,512]{2,1,0:T(8,128)}, u32[]{:S(2)}) copy-start(f32[8,64,512]{2,1,0:T(8,128)} %state_ref.1) | copy-start | bytes 3145732
  38.6 0.7 copy-start.12
  39.5 0.7 copy-start.13
  40.4 0.7 copy-start.5
  40.4 0.7 copy-start.6
  40.4 0.7 copy-start.7
  40.5 0.9 copy-start.1
  40.5 0.9 copy-start.2
  40.5 0.9 copy-start.3
  40.5 0.9 %copy-start.4 = (f32[128,128]{1,0:T(8,128)S(1)}, f32[128,128]{1,0:T(8,128)}, u32[]{:S(2)}) copy-start(f32[128,128]{1,0:T(8,128)} %constant.119.clone.turn_sin) | copy-start | bytes 196612
